TPU v7x, 256 devices: a whole 4x4x8 slice. The times are simulated.
256 devices in a mesh: dp: 2 (over x_lo), ctx: 16 (over z, core), exp: 8 (over y, x_hi).
Axes of the slice: x: 4 (x_hi: 2, x_lo: 2; x = x_hi * 2 + x_lo), y: 4, z: 8, core: 2. Of those that a mesh axis runs over, the one named last changes fastest.
Arguments:
- queries: bfloat16 [512, 6144], P(('dp', 'ctx'), 'exp'), parts along dimension 0, may hold values from -150 to 150
- span_keys: bfloat16 [512, 1024], P(('dp', 'ctx'), 'exp'), parts along dimension 0, may hold values from -5 to 5
- span_values: bfloat16 [512, 1024], P(('dp', 'ctx'), 'exp'), parts along dimension 0, may hold values from -5 to 5
- cache_keys: bfloat16 [131072, 1024], P(('dp', 'ctx'), 'exp'), parts along dimension 0, may hold values from -5 to 5
- cache_values: bfloat16 [131072, 1024], P(('dp', 'ctx'), 'exp'), parts along dimension 0, may hold values from -5 to 5
- span_start: int32 [2], P('dp'), parts along dimension 0, may hold values from 16384 to 65536
- residual: bfloat16 [512, 6144], P(('dp', 'ctx', 'exp')), parts along dimension 0, may hold values from -40 to 40
- out_weight: bfloat16 [6144, 6144], P('exp', 'ctx'), may hold values from -0.078125 to 0.078125
- norm_gain: bfloat16 [6144], replicated, may hold values from 0.099609375 to 1.8984375
- router_weight: bfloat16 [6144, 4], replicated, may hold values from -0.078125 to 0.078125
- expert_ids: int32 [512, 2], P('dp'), parts along dimension 0, may hold values from 0 to 3, as said below
- gate_weight: bfloat16 [6144, 32768], P(None, ('ctx', 'exp')), may hold values from -0.078125 to 0.078125
- up_weight: bfloat16 [6144, 32768], P(None, ('ctx', 'exp')), may hold values from -0.078125 to 0.078125
- down_weight: bfloat16 [32768, 6144], P(('ctx', 'exp')), may hold values from -0.0625 to 0.0625
Outputs:
- mixed: bfloat16 [512, 6144], P(('dp', 'ctx', 'exp')), parts along dimension 0
There are 2 independent parts, one for each index of `dp`. A program takes and returns all parts, laid end to end along the dimension named above; an argument that names none is the same for every part. Nothing has to cross between parts.
Inputs may be any that keep to these rules, and one draw needn't show every extreme that they name: `expert_ids`: the two experts of a token differ.
All inputs are finite; a program needn't handle non-finite values.
Results may differ from a plain program's by a relative error of at most 0.013.
Values may be sent and summed in bfloat16 or wider, within the bound.
No kernel may reach another device: no remote copies, remote signals or barrier semaphores. Data moves between devices by JAX's collectives and lax.ppermute only.
A program may use at most 128 MiB of HBM per device.

v0:
```python
import math

import jax
import jax.numpy as jnp
from jax import lax
from jax.sharding import PartitionSpec as P

D = 6144
HEAD_DIM = 128
EXPERTS = 4
FF = 8192
TOPK = 2
SPAN = 256
CAP = 160


EPSILON = 1e-05
MASKED = -1e30


def combined_all(shard, axis, join):
    gathered = jax.tree.map(
        lambda a, kind: lax.all_gather(a.astype(kind), axis),
        shard,
        jax.tree.map(lambda a: jnp.bfloat16 if a.dtype == jnp.float32 else a.dtype, shard),
    )

    def take(source):
        return jax.tree.map(
            lambda a, own: lax.dynamic_index_in_dim(a, source, 0, False).astype(own.dtype),
            gathered,
            shard,
        )

    return lax.fori_loop(
        1, lax.axis_size(axis), lambda source, state: join(state, take(source)), take(0)
    )


def partial_softmax(query_block, key_block, value_block, allowed):
    scale = query_block.shape[3] ** (-0.5)
    scores = (
        jnp.einsum("rkgd,lkd->rkgl", query_block, key_block, preferred_element_type=jnp.float32)
        * scale
    )
    scores = jnp.where(allowed[:, None, None, :], scores, MASKED)
    peaks = jnp.max(scores, axis=3)
    weights = jnp.where(allowed[:, None, None, :], jnp.exp(scores - peaks[..., None]), 0.0)
    masses = jnp.sum(weights, axis=3)
    carried = jnp.einsum(
        "rkgl,lkd->rkgd",
        weights.astype(jnp.bfloat16),
        value_block,
        preferred_element_type=jnp.float32,
    )
    return (peaks, masses, carried)


def combine_parts(earlier, later):
    peaks = jnp.maximum(earlier[0], later[0])
    early_factor = jnp.exp(earlier[0] - peaks)
    late_factor = jnp.exp(later[0] - peaks)
    masses = earlier[1] * early_factor + later[1] * late_factor
    carried = earlier[2] * early_factor[..., None] + later[2] * late_factor[..., None]
    return (peaks, masses, carried)


def empty_state(row_count, kv_local, per_group, head_dim):
    return (
        jnp.full((row_count, kv_local, per_group), MASKED, jnp.float32),
        jnp.zeros((row_count, kv_local, per_group), jnp.float32),
        jnp.zeros((row_count, kv_local, per_group, head_dim), jnp.float32),
    )


def cache_rule(limit, row_count):

    def allow(places):
        return jnp.broadcast_to((places < limit)[None, :], (row_count, places.shape[0]))

    return allow


def span_rule(query_places):

    def allow(places):
        return places[None, :] <= query_places[:, None]

    return allow


def scan_keys(running, query_block, key_rows, value_rows, first_row, allow):
    row_count, kv_local, per_group, head_dim = query_block.shape
    key_count = key_rows.shape[0]
    block_len = math.gcd(key_count, 1024)
    block_total = key_count // block_len
    key_blocks = key_rows.reshape(block_total, block_len, kv_local, head_dim)
    value_blocks = value_rows.reshape(block_total, block_len, kv_local, head_dim)

    def advance(state, block_item):
        block_keys, block_values, block_no = block_item
        places = first_row + block_no * block_len + jnp.arange(block_len, dtype=jnp.int32)
        return (
            combine_parts(
                state, partial_softmax(query_block, block_keys, block_values, allow(places))
            ),
            None,
        )

    return lax.scan(
        advance, running, (key_blocks, value_blocks, jnp.arange(block_total, dtype=jnp.int32))
    )[0]


def local_attention(
    query_block,
    query_places,
    cache_keys,
    cache_values,
    cache_first,
    span_keys,
    span_values,
    span_first,
    limit,
):
    row_count, kv_local, per_group, head_dim = query_block.shape
    initial = empty_state(row_count, kv_local, per_group, head_dim)
    running = scan_keys(
        initial,
        query_block,
        cache_keys.reshape(cache_keys.shape[0], kv_local, head_dim),
        cache_values.reshape(cache_values.shape[0], kv_local, head_dim),
        cache_first,
        cache_rule(limit, row_count),
    )
    return scan_keys(
        running,
        query_block,
        span_keys.reshape(span_keys.shape[0], kv_local, head_dim),
        span_values.reshape(span_values.shape[0], kv_local, head_dim),
        span_first,
        span_rule(query_places),
    )


def shards(
    queries,
    span_keys,
    span_values,
    cache_keys,
    cache_values,
    span_start,
    residual,
    out_weight,
    norm_gain,
    router_weight,
    expert_ids,
    gate_weight,
    up_weight,
    down_weight,
):
    ctx_count = lax.axis_size("ctx")
    exp_count = lax.axis_size("exp")
    ctx_index = lax.axis_index("ctx")
    exp_index = lax.axis_index("exp")
    kv_local = cache_keys.shape[1] // HEAD_DIM
    per_group = queries.shape[1] // (kv_local * HEAD_DIM)
    shard_rows = queries.shape[0]
    limit = span_start[0]
    cache_first = ctx_index * cache_keys.shape[0]
    span_first = ctx_index * shard_rows
    all_places = jnp.arange(SPAN, dtype=jnp.int32)
    gathered = lax.all_gather(queries, "ctx", axis=0, tiled=True)
    softmax_state = local_attention(
        gathered.reshape(SPAN, kv_local, per_group, HEAD_DIM),
        all_places,
        cache_keys,
        cache_values,
        cache_first,
        span_keys,
        span_values,
        span_first,
        limit,
    )
    peaks, masses, carried = combined_all(softmax_state, "ctx", combine_parts)
    attended = (carried / masses[..., None]).astype(jnp.bfloat16).reshape(SPAN, -1)
    block_rows = SPAN // exp_count
    fine_rows = SPAN // (ctx_count * exp_count)
    ctx_rows = SPAN // ctx_count
    row_order = jnp.arange(block_rows * lax.axis_size("exp"), dtype=jnp.int32)
    exp_part = row_order // block_rows
    within = row_order % block_rows
    tokens = within // fine_rows * ctx_rows + exp_part * fine_rows + within % fine_rows
    projected = lax.psum_scatter(
        jnp.dot(attended[tokens], out_weight, preferred_element_type=jnp.float32).astype(
            jnp.bfloat16
        ),
        "exp",
        scatter_dimension=0,
        tiled=True,
    ).astype(jnp.float32)
    projected = lax.all_to_all(
        projected.astype(jnp.bfloat16), "ctx", split_axis=0, concat_axis=1, tiled=True
    ).astype(projected.dtype)
    mid = (residual.astype(jnp.float32) + projected).astype(jnp.bfloat16)
    mid_wide = mid.astype(jnp.float32)
    scale_rows = lax.rsqrt(jnp.mean(mid_wide * mid_wide, axis=1, keepdims=True) + EPSILON)
    normed = (mid_wide * scale_rows * norm_gain.astype(jnp.float32)).astype(jnp.bfloat16)
    all_normed = lax.all_gather(normed, ("ctx", "exp"), axis=0, tiled=True)
    logits = jnp.dot(all_normed, router_weight, preferred_element_type=jnp.float32)
    one_hot = expert_ids[:, :, None] == jnp.arange(EXPERTS, dtype=jnp.int32)[None, None, :]
    picked = jnp.sum(jnp.where(one_hot, logits[:, None, :], 0.0), axis=2)
    gate_vals = 1.0 / (1.0 + jnp.exp(picked[:, ::-1] - picked))
    pair_hot = one_hot.reshape(SPAN * TOPK, EXPERTS).astype(jnp.int32)
    earlier_count = jnp.cumsum(pair_hot, axis=0) - pair_hot
    pair_slot = jnp.sum(earlier_count * pair_hot, axis=1)
    slot_of = pair_slot.reshape(SPAN, TOPK)
    is_kept = slot_of < CAP
    units = gate_weight.shape[1]
    expert = (ctx_index * exp_count + exp_index) * units // FF
    pair_expert = expert_ids.reshape(-1)
    pair_token = jnp.arange(SPAN * TOPK, dtype=jnp.int32) // TOPK
    match = (pair_expert == expert)[None, :] & (
        pair_slot[None, :] == jnp.arange(CAP, dtype=jnp.int32)[:, None]
    )
    slot_token = jnp.sum(jnp.where(match, pair_token[None, :], 0), axis=1)
    slot_live = jnp.any(match, axis=1)
    slot_inputs = jnp.where(slot_live[:, None], all_normed[slot_token], jnp.zeros((), jnp.bfloat16))
    gate_part = jnp.dot(slot_inputs, gate_weight, preferred_element_type=jnp.float32)
    up_part = jnp.dot(slot_inputs, up_weight, preferred_element_type=jnp.float32)
    hidden = (jax.nn.silu(gate_part) * up_part).astype(jnp.bfloat16)
    partial_out = jnp.dot(hidden, down_weight, preferred_element_type=jnp.float32)
    tokens = jnp.arange(fine_rows * lax.axis_size(("ctx", "exp")), dtype=jnp.int32)
    result = jnp.zeros((fine_rows * lax.axis_size(("ctx", "exp")), D), jnp.float32)
    for pick_no in range(TOPK):
        in_use = (expert_ids[tokens, pick_no] == expert) & is_kept[tokens, pick_no]
        slot_idx = jnp.clip(slot_of[tokens, pick_no], 0, CAP - 1)
        result = result + jnp.where(
            in_use[:, None], gate_vals[tokens, pick_no][:, None] * partial_out[slot_idx], 0.0
        )
    expert_sum = lax.psum_scatter(result, ("ctx", "exp"), scatter_dimension=0, tiled=True)
    return (mid.astype(jnp.float32) + expert_sum).astype(jnp.bfloat16)


def solution(mesh):
    placed = (
        P(("dp", "ctx"), "exp"),
        P(("dp", "ctx"), "exp"),
        P(("dp", "ctx"), "exp"),
        P(("dp", "ctx"), "exp"),
        P(("dp", "ctx"), "exp"),
        P("dp"),
        P(("dp", "ctx", "exp"), None),
        P("exp", "ctx"),
        P(),
        P(),
        P("dp", None),
        P(None, ("ctx", "exp")),
        P(None, ("ctx", "exp")),
        P(("ctx", "exp"), None),
    )
    return jax.shard_map(
        shards, mesh=mesh, in_specs=placed, out_specs=P(("dp", "ctx", "exp"), None), check_vma=False
    )
```

profile of v0, /device:TPU:2, one launch (start us, length us, event | category | flops | bytes accessed | tf_op | source)
XLA Modules:
  0.0 1772.5 jit_solution(358080718160837593)
XLA Ops:
  7.2 21.4 %all_gather.24 = bf16[256,768]{1,0:T(8,128)(2,1)S(1)} all-gather(bf16[16,768]{1,0:T(8,128)(2,1)} %param.18), channel_id=1, replica_groups=mesh['dp'=2,'ctx'=16,'exp'=8] {'ctx'}, dimensions={0}, use_global_device_ids=true | all-gather | bytes 417792 | tf_op jit(solution)/shard_map/all_gather | solution.py:173
  31.2 41.3 %while.41 = (s32[]{:T(128)}, f32[256,1,6]{0,2,1:T(8,128)S(1)}, f32[256,1,6]{0,2,1:T(8,128)}, f32[256,1,6,128]{0,3,2,1:T(8,128)}, s32[4]{0:T(128)}, /*index=5*/s3...) while((s32[]{:T(128)}, f32[256,1,6]{0,2,1:T(8,128)S(1)}, ...), condition=%wide.region_3.4_spmd.clone, body=%wide.region_0.3_spmd.clone.sunk | while | flops 826554368 | bytes 27833652 | solution.py:110
  37.9 2.8 fusion.121
  48.2 2.8 fusion.121
  58.6 2.8 fusion.121
  68.9 2.8 fusion.121
  72.6 2.3 copy.119
  77.5 2.5 fusion.45
  80.1 14.6 all-gather
  94.8 16.1 all-gather.1
  110.9 13.8 all-gather.7.cloned.1.call-done
  127.3 72.2 %while.40 = (s32[]{:T(128)}, f32[256,1,6]{0,1,2:T(1,128)S(1)}, f32[256,1,6]{0,1,2:T(1,128)S(1)}, f32[256,1,6,128]{3,2,1,0:T(8,128)}, bf16[16,256,1,6]{1,0,3,2:T(...) while((s32[]{:T(128)}, f32[256,1,6]{0,1,2:T(1,128)S(1)}, ...), condition=%wide.region_7.8_spmd, body=%wide.region_6.7_spmd.sunk | while | flops 798725 | bytes 2832527 | solution.py:35
  128.7 3.4 fusion.115
  133.5 3.4 fusion.115
  138.3 3.4 fusion.115
  143.1 3.4 fusion.115
  147.9 3.4 fusion.115
  152.7 3.4 fusion.115
  157.6 3.4 fusion.115
  162.4 3.4 fusion.115
  167.2 3.4 fusion.115
  172.0 3.4 fusion.115
  176.8 3.4 fusion.115
  181.6 3.4 fusion.115
  186.4 3.4 fusion.115
  191.2 3.4 fusion.115
  196.0 3.4 fusion.115
  199.5 2.4 copy.126
  206.9 2.2 convolution_convert_fusion
  209.2 72.8 %reduce-scatter.2.cloned.1.call-done = bf16[32,384]{1,0:T(8,128)(2,1)} async-done(((bf16[256,384]{1,0:T(8,128)(2,1)}), bf16[32,384]{1,0:T(8,128)(2,1)}) %reduce-scatter.2.cloned.1.call-update) | async-done | bytes 24592 | tf_op jit(solution)/shard_map/reduce_scatter | solution.py:194
  283.3 7.1 all-to-all-start
  291.2 6.9 all-to-all-done
  300.4 2.5 gather_fusion.1
  302.9 2.5 gather_fusion.7
  311.2 2.5 gather_fusion.8
  313.7 2.5 gather_fusion.2
  316.6 94.2 %all-gather.9.cloned.1.call-done = bf16[128,2,6144]{2,1,0:T(2,128)(2,1)} async-done(((bf16[1,2,6144]{2,1,0:T(2,128)(2,1)}), bf16[128,2,6144]{2,1,0:T(2,128)(2,1)}) %all-gather.9.cloned.1.call-update) | async-done | bytes 3145744 | tf_op jit(solution)/shard_map/all_gather | solution.py:209
  410.8 7.3 reshape.576
  418.1 2.8 fusion.97
  421.1 2.5 gather_fusion.3
  423.6 2.7 gather_fusion.9
  426.3 7.2 gather_fusion.4
  433.5 3.2 fusion.50
  436.7 6.7 fusion.49
  443.4 9.9 gather_fusion.11
  453.3 10.2 gather_fusion.6
  463.5 7.2 select_add_fusion
  472.6 1291.8 %all-reduce.3.cloned.1.call-done = f32[256,6144]{1,0:T(8,128)} async-done(((f32[256,6144]{1,0:T(8,128)}), f32[256,6144]{1,0:T(8,128)}) %all-reduce.3.cloned.1.call-update) | async-done | bytes 6291472
  (202 shorter events, 74.6 us)
Async XLA Ops:
  6.5 430.2 %copy-start = (bf16[256,6144]{1,0:T(8,128)(2,1)S(1)}, bf16[256,6144]{1,0:T(8,128)(2,1)}, u32[]{:S(2)}) copy-start(bf16[256,6144]{1,0:T(8,128)(2,1)} %param.31) | copy-start | bytes 9437188
  6.5 118.2 %all-gather.7.cloned.1.call-start = ((), (), s32[]{:S(2)}) async-start(), calls=%async_computation.3 | async-start | bytes 6684672 | tf_op jit(solution)/shard_map/all_gather | solution.py:23
  33.8 4.1 copy-start.5
  33.8 4.1 copy-start.3
  37.9 2.8 copy-start.6
  40.7 0.9 copy-start.4
  44.1 4.1 copy-start.5
  44.1 4.1 copy-start.3
  48.2 2.8 copy-start.6
  51.0 0.9 copy-start.4
  54.4 4.1 copy-start.5
  54.4 4.1 copy-start.3
  58.5 2.8 copy-start.6
  61.4 0.9 copy-start.4
  64.7 4.1 copy-start.5
  64.8 4.1 copy-start.3
  68.9 2.8 copy-start.6
  71.7 0.9 copy-start.4
  80.0 201.9 %reduce-scatter.2.cloned.1.call-start = ((), (), s32[]{:S(2)}) async-start(), calls=%async_computation.2 | async-start | bytes 221184 | tf_op jit(solution)/shard_map/reduce_scatter | solution.py:194
  199.5 100.5 %copy-start.1 = (s32[256,2]{0,1:T(2,128)S(1)}, s32[256,2]{0,1:T(2,128)}, u32[]{:S(2)}) copy-start(s32[256,2]{0,1:T(2,128)} %param.28) | copy-start | bytes 6148
  199.5 103.4 %copy-start.2 = (s32[256]{0:T(256)S(1)}, s32[256]{0:T(256)}, u32[]{:S(2)}) copy-start(s32[256]{0:T(256)} %constant.372) | copy-start | bytes 3076
  283.3 14.8 all-to-all-start
  290.4 120.4 %all-gather.9.cloned.1.call-start = ((), (), s32[]{:S(2)}) async-start(), calls=%async_computation.4 | async-start | bytes 3170304 | tf_op jit(solution)/shard_map/all_gather | solution.py:209
  299.7 1464.7 %all-reduce.3.cloned.1.call-start = ((), (), s32[]{:S(2)}) async-start(), calls=%async_computation.5 | async-start | bytes 12582912
  300.4 117.7 %copy-start.7 = (bf16[6144,4]{0,1:T(4,128)(2,1)S(1)}, bf16[6144,4]{0,1:T(4,128)(2,1)}, u32[]{:S(2)}) copy-start(bf16[6144,4]{0,1:T(4,128)(2,1)} %param.27) | copy-start | bytes 147460
  470.7 0.7 copy-start.8
Sparse Core Ops, SparseCore 0:
  80.2 44.5 all-gather.6
  209.3 72.5 reduce-scatter.1
  299.9 110.9 all-gather.8
  470.8 1293.5 all-reduce.2
where the time goes:
time: 1770 us
  waiting for transfers between devices  1480 us (84%)
  local copies, waits for them, and re-layouts  96.9 us (5%)
  other arithmetic  81.1 us (5%)
  blocking collectives  52.1 us (3%)
  matrix products  37.9 us (2%)
    unnamed x5, waiting for transfers between devices  1290 us
    all_gather x1, waiting for transfers between devices, shards(): all_normed = lax.all_gather(normed, ('ctx', 'exp'), axis=0, tiled=True)  94.2 us
    reduce_scatter x1, waiting for transfers between devices, shards(): lax.psum_scatter(jnp.dot(attended[tokens], out_weight, preferred_element_...  72.8 us
    add x15, other arithmetic, combine_parts(): earlier[2] * early_factor[..., None] + later[2] * late_factor[..., None]  51.7 us
  transfers between devices with their start and end apart: 5, of which 5 were waited for; matrix products, arithmetic and copies ran while one was open for 1% of the time, Pallas kernels for 0%

commit v1 on v0

v1 whole, which is shorter than its diff:
```python
import math

import jax
import jax.numpy as jnp
from jax import lax
from jax.experimental import pallas as pl
from jax.experimental.pallas import tpu as pltpu
from jax.sharding import PartitionSpec as P

D = 6144
HEAD_DIM = 128
EXPERTS = 4
FF = 8192
TOPK = 2
SPAN = 256
CAP = 160
NZ = 8
NE = 8
FINE = 2
HEADS_LOCAL = 6
BLOCK_TOKENS = 16
BLOCK_ROWS = BLOCK_TOKENS * HEADS_LOCAL
ROWS = NZ * BLOCK_ROWS
Q_BLOCK = 256
CHUNK = 4096
MASKED_CHUNK = 1024
MESSAGE_ROWS = BLOCK_ROWS + 16
COLS = 768
HALF = 384
EPSILON = 1e-05
MASKED = -1e30
EXP2_SCALE = HEAD_DIM**-0.5 * math.log2(math.e)
BF16 = jnp.bfloat16
F32 = jnp.float32

Z_GROUPS = [[2 * z + core for z in range(NZ)] for core in range(2)]
SIBLINGS = [(c, c ^ 1) for c in range(2 * NZ)]


def exchange_z(blocks):
    return lax.all_to_all(blocks, "ctx", 0, 0, axis_index_groups=Z_GROUPS, tiled=True)


def exchange_exp(blocks):
    return lax.all_to_all(blocks, "exp", 0, 0, tiled=True)


def sibling(x):
    return lax.ppermute(x, "ctx", SIBLINGS)


VMEM = pl.BlockSpec(memory_space=pltpu.VMEM)
SMEM = pl.BlockSpec(memory_space=pltpu.SMEM)
ANY = pl.BlockSpec(memory_space=pl.ANY)


def call(kernel, shape, *args, specs=None, dtype=BF16, limit=32, flops=1 << 20, scratch=()):
    return pl.pallas_call(
        kernel,
        out_shape=jax.ShapeDtypeStruct(shape, dtype),
        in_specs=specs or [VMEM] * len(args),
        out_specs=VMEM,
        scratch_shapes=scratch,
        compiler_params=pltpu.CompilerParams(vmem_limit_bytes=limit << 20),
        cost_estimate=pl.CostEstimate(flops=flops, bytes_accessed=1 << 20, transcendentals=0),
    )(*args)


def first_message_kernel(q, residual, out):
    res = residual[...].astype(F32)
    row = lax.broadcasted_iota(jnp.int32, (16, HEAD_DIM), 0)
    for z in range(NZ):
        for h in range(HEADS_LOCAL):
            out[z, h * BLOCK_TOKENS : (h + 1) * BLOCK_TOKENS, :] = q[
                :, h * HEAD_DIM : (h + 1) * HEAD_DIM
            ]
        rows = jnp.zeros((16, HEAD_DIM), F32)
        for j in range(COLS // HEAD_DIM):
            start = z * COLS + j * HEAD_DIM
            piece = res[:, start : start + HEAD_DIM]
            for f in range(FINE):
                rows = jnp.where(row == j * FINE + f, piece[f : f + 1, :], rows)
        out[z, BLOCK_ROWS:, :] = rows.astype(BF16)


def split3(x):
    first = x.astype(BF16).astype(F32)
    rest = x - first
    second = rest.astype(BF16).astype(F32)
    return first, second, rest - second


def attention_kernel(
    info, first, k0, v0, k1, v1, sk, sv, out, q, keys, values, peak, carried, sems
):
    copies = []
    for i, (source, target) in enumerate(((k0, keys), (v0, values), (k1, keys), (v1, values))):
        place = pl.ds(i // 2 * CHUNK, CHUNK)
        copies.append(pltpu.make_async_copy(source, target.at[place, :], sems.at[i]))
        copies[i].start()
    q[...] = first[:, :BLOCK_ROWS, :].reshape(ROWS, HEAD_DIM)
    blocks = ROWS // Q_BLOCK

    def columns(b):
        return slice(b * Q_BLOCK, (b + 1) * Q_BLOCK)

    def scores_of(rows, b):
        return lax.dot_general(
            rows, q[columns(b), :], (((1,), (1,)), ((), ())), preferred_element_type=F32
        )

    def with_ones(rows):
        return jnp.concatenate([rows.T, jnp.ones((16, rows.shape[0]), BF16)], axis=0)

    core = info[2]
    span_rows = 2 * BLOCK_TOKENS
    span_values = with_ones(sv[...])
    for b in range(blocks):
        row = lax.broadcasted_iota(jnp.int32, (span_rows, Q_BLOCK), 0)
        col = lax.broadcasted_iota(jnp.int32, (span_rows, Q_BLOCK), 1) + b * Q_BLOCK
        token = col // BLOCK_ROWS * span_rows + core * BLOCK_TOKENS + col % BLOCK_TOKENS
        allowed = info[3] + row <= token
        s = jnp.where(allowed, scores_of(sk[...], b), MASKED)
        top = jnp.max(s, axis=0, keepdims=True)
        w = jnp.where(allowed, jnp.exp2((s - top) * EXP2_SCALE), 0.0).astype(BF16)
        peak[:, columns(b)] = jnp.broadcast_to(top, (8, Q_BLOCK))
        carried[:, columns(b)] = jnp.dot(span_values, w, preferred_element_type=F32)

    def soften(s, b):
        before = peak[:1, columns(b)]
        top = jnp.maximum(before, jnp.max(s, axis=0, keepdims=True))
        peak[:, columns(b)] = jnp.broadcast_to(top, (8, Q_BLOCK))
        w = jnp.exp2((s - top) * EXP2_SCALE).astype(BF16)
        return w, jnp.exp2((before - top) * EXP2_SCALE)

    def gather(b, w, factor, rows):
        carried[:, columns(b)] = carried[:, columns(b)] * factor + jnp.dot(
            rows, w, preferred_element_type=F32
        )

    for part in range(2):
        valid = info[part]
        copies[2 * part].wait()
        copies[2 * part + 1].wait()

        @pl.when(valid == CHUNK)
        def _(part=part):
            place = slice(part * CHUNK, (part + 1) * CHUNK)
            key_rows = keys[place, :]
            value_rows = with_ones(values[place, :])
            s = scores_of(key_rows, 0)
            earlier = None
            for b in range(blocks):
                later = scores_of(key_rows, b + 1) if b + 1 < blocks else None
                current = soften(s, b)
                if earlier is not None:
                    gather(b - 1, *earlier, value_rows)
                earlier, s = current, later
            gather(blocks - 1, *earlier, value_rows)

        @pl.when(valid < CHUNK)
        def _(part=part, valid=valid):
            @pl.loop(0, (valid + MASKED_CHUNK - 1) // MASKED_CHUNK)
            def _(j):
                start = pl.multiple_of(part * CHUNK + j * MASKED_CHUNK, MASKED_CHUNK)
                key_rows = keys[pl.ds(start, MASKED_CHUNK), :]
                value_rows = with_ones(values[pl.ds(start, MASKED_CHUNK), :])
                row = lax.broadcasted_iota(jnp.int32, (MASKED_CHUNK, Q_BLOCK), 0)
                for b in range(blocks):
                    s = scores_of(key_rows, b)
                    s = jnp.where(row + j * MASKED_CHUNK < valid, s, MASKED)
                    gather(b, *soften(s, b), value_rows)

    rows = carried[:HEAD_DIM, :].T.astype(BF16)
    out[:, :BLOCK_ROWS, :] = rows.reshape(NZ, BLOCK_ROWS, HEAD_DIM)
    terms = split3(peak[:1, :]) + split3(carried[HEAD_DIM : HEAD_DIM + 1, :])
    row = lax.broadcasted_iota(jnp.int32, (16, ROWS), 0)
    stats = jnp.zeros((16, ROWS), F32)
    for i, term in enumerate(terms):
        stats = jnp.where(row == i, term, stats)
    for z in range(NZ):
        turned = stats if z == 0 else pltpu.roll(stats, ROWS - z * BLOCK_ROWS, 1)
        out[z, BLOCK_ROWS:, :] = turned[:, :HEAD_DIM].astype(BF16)


def combine_kernel(message, out):
    peaks, masses = [], []
    for z in range(NZ):
        r = message[z, BLOCK_ROWS:, :].astype(F32)
        peaks.append(r[0:1] + r[1:2] + r[2:3])
        masses.append(r[3:4] + r[4:5] + r[5:6])
    top = peaks[0]
    for z in range(1, NZ):
        top = jnp.maximum(top, peaks[z])
    factors = [jnp.exp2((p - top) * EXP2_SCALE) for p in peaks]
    total = factors[0] * masses[0]
    for z in range(1, NZ):
        total = total + factors[z] * masses[z]
    row = lax.broadcasted_iota(jnp.int32, (HEAD_DIM, HEAD_DIM), 0)
    shares = jnp.zeros((HEAD_DIM, HEAD_DIM), F32)
    for z in range(NZ):
        shares = jnp.where(row == z, factors[z] / total, shares)
    shares = shares.T
    rows = jnp.zeros((BLOCK_ROWS, HEAD_DIM), F32)
    for z in range(NZ):
        rows = rows + message[z, :BLOCK_ROWS, :].astype(F32) * shares[:BLOCK_ROWS, z : z + 1]
    rows = rows.astype(BF16)
    for h in range(HEADS_LOCAL):
        piece = rows[h * BLOCK_TOKENS : (h + 1) * BLOCK_TOKENS]
        for z in range(NZ):
            out[z, :, h * HEAD_DIM : (h + 1) * HEAD_DIM] = piece


def project_kernel(info, x, own, other, out):
    r = lax.broadcasted_iota(jnp.int32, (128, 128), 0)
    c = lax.broadcasted_iota(jnp.int32, (128, 128), 1)
    wanted = r % 16 // FINE * 16 + r // 16 * FINE + r % FINE
    turn = jnp.where(c == wanted, 1.0, 0.0).astype(BF16)
    rows = jnp.dot(turn, x[...].reshape(128, COLS), preferred_element_type=F32).astype(BF16)
    core = info[2]
    for weight, side in ((own, core), (other, 1 - core)):
        part = jnp.dot(rows, weight[...], preferred_element_type=F32).astype(BF16)
        out[:, :, pl.ds(pl.multiple_of(side * HALF, HALF), HALF)] = part.reshape(NE, 16, HALF)


def mid_kernel(parts, message, out):
    total = parts[0].astype(F32)
    for e in range(1, NE):
        total = total + parts[e].astype(F32)
    rows = message[:, BLOCK_ROWS:, :].reshape(128, HEAD_DIM)
    r = lax.broadcasted_iota(jnp.int32, (16, 128), 0)
    c = lax.broadcasted_iota(jnp.int32, (16, 128), 1)
    for j in range(COLS // HEAD_DIM):
        pick = jnp.where(c == r // FINE * 16 + j * FINE + r % FINE, 1.0, 0.0).astype(BF16)
        place = slice(j * HEAD_DIM, (j + 1) * HEAD_DIM)
        res = jnp.dot(pick, rows, preferred_element_type=F32)
        mid = (res + total[:, place]).astype(BF16)
        for z in range(NZ):
            out[z, :, place] = mid


def norm_kernel(info, parts, gain, out, own):
    squares = jnp.zeros((16, 1), F32)
    for z in range(NZ):
        wide = parts[z].astype(F32)
        squares = squares + jnp.sum(wide * wide, axis=1, keepdims=True)
    scale = lax.rsqrt(squares * (1.0 / D) + EPSILON)
    r = lax.broadcasted_iota(jnp.int32, (16, 16), 0)
    c = lax.broadcasted_iota(jnp.int32, (16, 16), 1)
    pick = jnp.where((c == info[4] * FINE + r) & (r < FINE), 1.0, 0.0).astype(BF16)
    for z in range(NZ):
        place = slice(z * COLS, (z + 1) * COLS)
        mid = parts[z]
        normed = (mid.astype(F32) * scale * gain[:, place].astype(F32)).astype(BF16)
        for e in range(NE):
            out[e, :, place] = normed
        own[:, place] = jnp.dot(pick, mid, preferred_element_type=F32).astype(BF16)


MOE_STEPS = 8
MOE_TILE = D // MOE_STEPS


def moe_kernel(
    info, x, ids, router, g0, g1, u0, u1, d0, d1, out, gate, up, logits, hidden, share
):
    step = pl.program_id(0)
    units = g0.shape[1]

    @pl.when(step == 0)
    def _():
        gate[...] = jnp.zeros(gate.shape, F32)
        up[...] = jnp.zeros(up.shape, F32)
        logits[...] = jnp.zeros(logits.shape, F32)

    @pl.when(step < MOE_STEPS)
    def _():
        place = pl.ds(pl.multiple_of(step * MOE_TILE, MOE_TILE), MOE_TILE)
        rows = x[:, :, place].reshape(128, MOE_TILE)
        for i, (g, u) in enumerate(((g0, u0), (g1, u1))):
            side = slice(i * units, (i + 1) * units)
            gate[:, side] += jnp.dot(rows, g[...], preferred_element_type=F32)
            up[:, side] += jnp.dot(rows, u[...], preferred_element_type=F32)
        logits[...] += lax.dot_general(
            rows, router[:, place], (((1,), (1,)), ((), ())), preferred_element_type=F32
        )

    @pl.when(step == MOE_STEPS - 1)
    def _():
        g = gate[...]
        hidden[...] = (g / (1.0 + jnp.exp(-g)) * up[...]).astype(BF16)
        core, expert = info[2], info[5]
        r = lax.broadcasted_iota(jnp.int32, (128, SPAN), 0)
        u = lax.broadcasted_iota(jnp.int32, (128, SPAN), 1)
        token = (r % 16 // FINE * 2 + core) * BLOCK_TOKENS + r // 16 * FINE + r % FINE
        leading, trailing = ids[0:1, :], ids[1:2, :]
        chosen = (leading == expert) | (trailing == expert)
        other = jnp.where(leading == expert, trailing, leading)
        earlier = jnp.sum(jnp.where(chosen & (u < token), 1.0, 0.0), axis=1, keepdims=True)
        mine = jnp.sum(jnp.where(chosen & (u == token), 1.0, 0.0), axis=1, keepdims=True)
        other_id = jnp.sum(jnp.where(u == token, other.astype(F32), 0.0), axis=1, keepdims=True)
        lane = lax.broadcasted_iota(jnp.int32, logits.shape, 1)
        values = logits[...]
        own_logit = jnp.sum(jnp.where(lane == expert, values, 0.0), axis=1, keepdims=True)
        other_logit = jnp.sum(
            jnp.where(lane.astype(F32) == other_id, values, 0.0), axis=1, keepdims=True
        )
        active = (mine > 0.5) & (earlier < CAP - 0.5)
        share[...] = jnp.broadcast_to(
            jnp.where(active, 1.0 / (1.0 + jnp.exp(other_logit - own_logit)), 0.0), share.shape
        )

    @pl.when(step >= MOE_STEPS)
    def _():
        total = jnp.dot(hidden[:, :units], d0[...], preferred_element_type=F32)
        total = total + jnp.dot(hidden[:, units:], d1[...], preferred_element_type=F32)
        out[...] = (total * share[:, :1]).astype(BF16).reshape(NE, 16, MOE_TILE)


def experts(info, x, ids, router, g0, g1, u0, u1, d0, d1):
    units = g0.shape[1]
    wide = pl.BlockSpec((MOE_TILE, units), lambda i: (jnp.minimum(i, MOE_STEPS - 1), 0))
    down = pl.BlockSpec((units, MOE_TILE), lambda i: (0, jnp.maximum(i - MOE_STEPS, 0)))

    def whole(a):
        return pl.BlockSpec(a.shape, lambda i: (0,) * a.ndim)

    return pl.pallas_call(
        moe_kernel,
        grid=(2 * MOE_STEPS,),
        out_shape=jax.ShapeDtypeStruct((NE, 16, D), BF16),
        in_specs=[SMEM, whole(x), whole(ids), whole(router)] + [wide] * 4 + [down] * 2,
        out_specs=pl.BlockSpec(
            (NE, 16, MOE_TILE), lambda i: (0, 0, jnp.maximum(i - MOE_STEPS, 0))
        ),
        scratch_shapes=[
            pltpu.VMEM((128, 2 * units), F32),
            pltpu.VMEM((128, 2 * units), F32),
            pltpu.VMEM((128, 8), F32),
            pltpu.VMEM((128, 2 * units), BF16),
            pltpu.VMEM((128, 128), F32),
        ],
        compiler_params=pltpu.CompilerParams(vmem_limit_bytes=24 << 20),
        cost_estimate=pl.CostEstimate(
            flops=6 * 128 * D * 2 * units, bytes_accessed=22 << 20, transcendentals=128 * 512
        ),
    )(info, x, ids, router, g0, g1, u0, u1, d0, d1)


def sum_kernel(parts, out):
    total = parts[0].astype(F32)
    for e in range(1, NE):
        total = total + parts[e].astype(F32)
    for z in range(NZ):
        out[z] = total[z * FINE : (z + 1) * FINE].astype(BF16)


def last_kernel(parts, own, out):
    total = own[:, :].astype(F32)[:FINE]
    for z in range(NZ):
        total = total + parts[z].astype(F32)
    out[...] = total.astype(BF16)


def shards(
    queries,
    span_keys,
    span_values,
    cache_keys,
    cache_values,
    span_start,
    residual,
    out_weight,
    norm_gain,
    router_weight,
    expert_ids,
    gate_weight,
    up_weight,
    down_weight,
):
    ctx_index = lax.axis_index("ctx")
    core = ctx_index % 2
    z_index = ctx_index // 2
    key_rows = cache_keys.shape[0]

    other_keys = sibling(cache_keys)
    other_values = sibling(cache_values)
    span_own = jnp.concatenate([span_keys, span_values], axis=1)
    other_span = sibling(span_own)
    other_out = sibling(out_weight)
    other_gate = sibling(gate_weight)
    other_up = sibling(up_weight)
    other_down = sibling(down_weight)

    first = exchange_z(
        call(first_message_kernel, (NZ, MESSAGE_ROWS, HEAD_DIM), queries, residual)
    )

    def valid(index):
        return jnp.clip(span_start[0] - index * key_rows, 0, key_rows)

    own_first = core == 0
    span_both = jnp.concatenate(
        [jnp.where(own_first, span_own, other_span), jnp.where(own_first, other_span, span_own)], axis=0
    )
    info = jnp.stack(
        [
            valid(ctx_index),
            valid(ctx_index ^ 1),
            core,
            z_index * 2 * BLOCK_TOKENS,
            z_index,
            z_index // 2,
        ]
    ).astype(jnp.int32)
    second = exchange_z(
        call(
            attention_kernel,
            (NZ, MESSAGE_ROWS, HEAD_DIM),
            info,
            first,
            cache_keys,
            cache_values,
            other_keys,
            other_values,
            span_both[:, :HEAD_DIM],
            span_both[:, HEAD_DIM:],
            specs=[SMEM, VMEM, ANY, ANY, ANY, ANY, VMEM, VMEM],
            limit=48,
            flops=4 * ROWS * 2 * CHUNK * HEAD_DIM,
            scratch=[
                pltpu.VMEM((ROWS, HEAD_DIM), BF16),
                pltpu.VMEM((2 * CHUNK, HEAD_DIM), BF16),
                pltpu.VMEM((2 * CHUNK, HEAD_DIM), BF16),
                pltpu.VMEM((8, ROWS), F32),
                pltpu.VMEM((HEAD_DIM + 16, ROWS), F32),
                pltpu.SemaphoreType.DMA((4,)),
            ],
        )
    )
    third = exchange_z(call(combine_kernel, (NZ, BLOCK_TOKENS, COLS), second))
    fourth = exchange_exp(
        call(
            project_kernel,
            (NE, 16, COLS),
            info,
            third,
            out_weight,
            other_out,
            specs=[SMEM, VMEM, VMEM, VMEM],
        )
    )
    fifth = exchange_z(call(mid_kernel, (NZ, 16, COLS), fourth, first))
    normed, own_mid = pl.pallas_call(
        norm_kernel,
        out_shape=(
            jax.ShapeDtypeStruct((NE, 16, D), BF16),
            jax.ShapeDtypeStruct((16, D), BF16),
        ),
        in_specs=[SMEM, VMEM, VMEM],
        out_specs=(VMEM, VMEM),
        compiler_params=pltpu.CompilerParams(vmem_limit_bytes=16 << 20),
        cost_estimate=pl.CostEstimate(flops=1 << 20, bytes_accessed=2 << 20, transcendentals=0),
    )(info, fifth, norm_gain.reshape(1, D))
    tokens = exchange_exp(normed)

    ids = jnp.pad(expert_ids.T, ((0, 8 - TOPK), (0, 0)))
    router = jnp.pad(router_weight.T, ((0, 8 - EXPERTS), (0, 0)))
    result = experts(
        info,
        tokens,
        ids,
        router,
        gate_weight,
        other_gate,
        up_weight,
        other_up,
        down_weight,
        other_down,
    )
    sixth = exchange_exp(result)
    seventh = exchange_z(call(sum_kernel, (NZ, FINE, D), sixth))
    return call(last_kernel, (FINE, D), seventh, own_mid)


def solution(mesh):
    placed = (
        P(("dp", "ctx"), "exp"),
        P(("dp", "ctx"), "exp"),
        P(("dp", "ctx"), "exp"),
        P(("dp", "ctx"), "exp"),
        P(("dp", "ctx"), "exp"),
        P("dp"),
        P(("dp", "ctx", "exp"), None),
        P("exp", "ctx"),
        P(),
        P(),
        P("dp", None),
        P(None, ("ctx", "exp")),
        P(None, ("ctx", "exp")),
        P(("ctx", "exp"), None),
    )
    return jax.shard_map(
        shards, mesh=mesh, in_specs=placed, out_specs=P(("dp", "ctx", "exp"), None), check_vma=False
    )
```

time: 1770 us -> 171 us (0.10)
  waiting for transfers between devices: 1480 us -> 54.1 us
  local copies, waits for them, and re-layouts: 96.9 us -> 13.3 us
  other arithmetic: 81.1 us -> 0.01 us
  matrix products: 37.9 us -> 0 us
  Pallas kernels: 0 us -> 30.6 us
    unnamed x5 -> x0, waiting for transfers between devices: 1290 us -> none
    all_gather x2 -> x0, waiting for transfers between devices: 108 us -> none  [the longest x1 94.2 us: shards(): all_normed = lax.all_gather(normed, ('ctx', 'exp'), axis=0, tiled=True)]
    reduce_scatter x1 -> x0, waiting for transfers between devices: 72.8 us -> none  [shards(): lax.psum_scatter(jnp.dot(attended[tokens], out_weight, preferred_element_...]
    add x32 -> x0, other arithmetic: 59.5 us -> none  [the longest x15 51.7 us: combine_parts(): earlier[2] * early_factor[..., None] + later[2] * late_factor[..., None]]
    all_gather x3 -> x0, blocking collectives: 52.1 us -> none  [the longest x2 30.7 us: combined_all(): lax.all_gather(a.astype(kind), axis)]
    gather x12 -> x0, local copies, waits for them, and re-layouts: 48.2 us -> none  [the longest x2 20.1 us: shards(): partial_out[slot_idx]]
    all_to_all x1 -> x5, waiting for transfers between devices: 6.89 us -> 54.1 us  [the longest x4 37.4 us: exchange_z(): lax.all_to_all(blocks, 'ctx', 0, 0, axis_index_groups=Z_GROUPS, tiled=True)]
    all_to_all x0 -> x3, blocking collectives: none -> 46.9 us  [the longest x2 34.7 us: exchange_exp(): return lax.all_to_all(blocks, 'exp', 0, 0, tiled=True)]
  transfers between devices with their start and end apart: 5 -> 12, of which waited for: 5 -> 5; matrix products, arithmetic and copies ran while one was open for 1% -> 1% of each run, Pallas kernels for 0% -> 10%
where the time goes in v1:
time: 171 us; the launch traced here: 170 us
  waiting for transfers between devices  54.1 us (32%)
  blocking collectives  46.9 us (27%)
  Pallas kernels  30.6 us (18%)
  starting transfers between devices  23.9 us (14%)
  local copies, waits for them, and re-layouts  13.3 us (8%)
    all_to_all x4, waiting for transfers between devices, exchange_z(): lax.all_to_all(blocks, 'ctx', 0, 0, axis_index_groups=Z_GROUPS, tiled=True)  37.4 us
    all_to_all x2, blocking collectives, exchange_exp(): return lax.all_to_all(blocks, 'exp', 0, 0, tiled=True)  34.7 us
    all_to_all x4, starting transfers between devices, exchange_z(): lax.all_to_all(blocks, 'ctx', 0, 0, axis_index_groups=Z_GROUPS, tiled=True)  18.7 us
    all_to_all x1, waiting for transfers between devices, exchange_exp(): return lax.all_to_all(blocks, 'exp', 0, 0, tiled=True)  16.7 us
    pallas_call x7, Pallas kernels, call(): pl.pallas_call(kernel, out_shape=jax.ShapeDtypeStruct(shape, dtype), in_s...  15.6 us
    pallas_call x1, Pallas kernels, experts(): pl.pallas_call(moe_kernel, grid=(2 * MOE_STEPS,), out_shape=jax.ShapeDtyp...  13 us
    unnamed x27, local copies, waits for them, and re-layouts  12.5 us
    all_to_all x1, blocking collectives, exchange_z(): lax.all_to_all(blocks, 'ctx', 0, 0, axis_index_groups=Z_GROUPS, tiled=True)  12.2 us
  transfers between devices with their start and end apart: 12, of which 5 were waited for; matrix products, arithmetic and copies ran while one was open for 1% of the time, Pallas kernels for 10%

profile of v1, /device:TPU:2, one launch (start us, length us, event | category | flops | bytes accessed | tf_op | source)
XLA Modules:
  0.0 169.7 jit_solution(6322975282494484964)
XLA Ops:
  0.0 0.0 collective-permute-start
  0.0 0.5 collective-permute-start.1
  0.5 0.7 copy-done.4
  1.3 0.7 copy-done.5
  2.0 0.8 shard_map.136
  2.7 8.5 %all-to-all-start = ((bf16[8,112,128]{2,1,0:T(8,128)(2,1)}), bf16[8,112,128]{2,1,0:T(8,128)(2,1)S(1)}, u32[]{:S(2)}, u32[]{:S(2)}) async-start(bf16[8,112,128]{2,1,0:T(8,128)(2,1)} %shard_map.136), calls=%async_computation | async-start | bytes 458752 | tf_op jit(solution)/shard_map/all_to_all | solution.py:41
  11.2 0.7 constant_dynamic-update-slice_fusion.1
  11.9 0.7 constant_dynamic-update-slice_fusion
  12.6 0.0 collective-permute-start.2
  12.6 0.5 collective-permute-start.4
  13.1 0.0 collective-permute-start.5
  13.8 0.1 stack.27.info
  13.9 0.0 collective-permute-done.2
  13.9 0.6 collective-permute-start.6
  14.4 8.1 %all-to-all-done.first.message = bf16[8,112,128]{2,1,0:T(8,128)(2,1)S(1)} async-done(((bf16[8,112,128]{2,1,0:T(8,128)(2,1)}), bf16[8,112,128]{2,1,0:T(8,128)(2,1)S(1)}, u32[]{:S(2)}, u32[]{:S(2)}) %all-to-all-start) | async-done | bytes 229408 | tf_op jit(solution)/shard_map/all_to_all | solution.py:41
  22.6 0.0 collective-permute-done.k1
  22.6 0.0 collective-permute-done.1.v1
  22.6 1.0 copy-done.8
  23.6 1.2 copy-done.6
  24.8 1.2 copy-done.7
  26.0 1.2 copy-done.9
  27.2 11.0 %shard_map.137 = bf16[8,112,128]{2,1,0:T(8,128)(2,1)} custom-call(s32[6]{0:T(128)S(1)} %stack.27.info, bf16[8,112,128]{2,1,0:T(8,128)(2,1)S(1)} %all-to-all-done.first.message, bf16[4096,128]{1,0:T(8,128)(2,1)S(1)} %copy-done.6, bf16[4096,128]{1,0:T(8,128)(2,1)S(1)} %copy-done.7, bf16[4096,128]{1,0:T(8,128)(2,1)S(1)} %collective-permute-done.k1, ...), custom_call_target="tpu_custom_call" | custom-call | flops 3221225472 | bytes 1048576 | tf_op jit(solution)/shard_map/pallas_call | solution.py:58
  38.2 0.0 copy-start.11
  38.2 3.4 %all-to-all-start.1 = ((bf16[8,112,128]{2,1,0:T(8,128)(2,1)}), bf16[8,112,128]{2,1,0:T(8,128)(2,1)S(1)}, u32[]{:S(2)}, u32[]{:S(2)}) async-start(bf16[8,112,128]{2,1,0:T(8,128)(2,1)} %shard_map.137), calls=%async_computation.1 | async-start | bytes 458752 | tf_op jit(solution)/shard_map/all_to_all | solution.py:41
  41.7 0.1 collective-permute-start.3
  41.8 9.9 %all-to-all-done.1.message = bf16[8,112,128]{2,1,0:T(8,128)(2,1)S(1)} async-done(((bf16[8,112,128]{2,1,0:T(8,128)(2,1)}), bf16[8,112,128]{2,1,0:T(8,128)(2,1)S(1)}, u32[]{:S(2)}, u32[]{:S(2)}) %all-to-all-start.1) | async-done | bytes 229408 | tf_op jit(solution)/shard_map/all_to_all | solution.py:41
  51.7 1.0 shard_map.138
  52.7 3.4 %all-to-all-start.2 = ((bf16[8,16,768]{2,1,0:T(8,128)(2,1)}), bf16[8,16,768]{2,1,0:T(8,128)(2,1)S(1)}, u32[]{:S(2)}, u32[]{:S(2)}) async-start(bf16[8,16,768]{2,1,0:T(8,128)(2,1)} %shard_map.138), calls=%async_computation.2 | async-start | bytes 393216 | tf_op jit(solution)/shard_map/all_to_all | solution.py:41
  56.1 0.0 copy-start.12
  56.2 0.0 copy-start.10
  56.2 9.7 %all-to-all-done.2.x = bf16[8,16,768]{2,1,0:T(8,128)(2,1)S(1)} async-done(((bf16[8,16,768]{2,1,0:T(8,128)(2,1)}), bf16[8,16,768]{2,1,0:T(8,128)(2,1)S(1)}, u32[]{:S(2)}, u32[]{:S(2)}) %all-to-all-start.2) | async-done | bytes 196640 | tf_op jit(solution)/shard_map/all_to_all | solution.py:41
  65.8 1.0 shard_map.139
  66.9 14.3 %all_to_all.40.parts = bf16[8,16,768]{2,1,0:T(8,128)(2,1)S(1)} all-to-all(bf16[8,16,768]{2,1,0:T(8,128)(2,1)S(1)} %shard_map.139), channel_id=1, replica_groups=mesh['dp'=2,'ctx'=16,'exp'=8] {'exp'}, dimensions={0} | all-to-all | bytes 393216 | tf_op jit(solution)/shard_map/all_to_all | solution.py:45
  81.2 0.9 shard_map.140
  82.0 3.4 %all-to-all-start.4 = ((bf16[8,16,768]{2,1,0:T(8,128)(2,1)}), bf16[8,16,768]{2,1,0:T(8,128)(2,1)S(1)}, u32[]{:S(2)}, u32[]{:S(2)}) async-start(bf16[8,16,768]{2,1,0:T(8,128)(2,1)} %shard_map.140), calls=%async_computation.4 | async-start | bytes 393216 | tf_op jit(solution)/shard_map/all_to_all | solution.py:41
  85.5 9.7 %all-to-all-done.4.parts = bf16[8,16,768]{2,1,0:T(8,128)(2,1)S(1)} async-done(((bf16[8,16,768]{2,1,0:T(8,128)(2,1)}), bf16[8,16,768]{2,1,0:T(8,128)(2,1)S(1)}, u32[]{:S(2)}, u32[]{:S(2)}) %all-to-all-start.4) | async-done | bytes 196640 | tf_op jit(solution)/shard_map/all_to_all | solution.py:41
  95.1 2.0 %shard_map.141 = (bf16[8,16,6144]{2,1,0:T(8,128)(2,1)}, bf16[16,6144]{1,0:T(8,128)(2,1)S(1)}) custom-call(s32[6]{0:T(128)S(1)} %stack.27.info, bf16[8,16,768]{2,1,0:T(8,128)(2,1)S(1)} %all-to-all-done.4.parts, bf16[1,6144]{1,0:T(2,128)(2,1)S(1)} %reshape.3.gain), custom_call_target="tpu_custom_call" | custom-call | flops 1048576 | bytes 2097152 | tf_op jit(solution)/shard_map/pallas_call | solution.py:454
  97.1 3.6 %all-to-all-start.5 = ((bf16[8,16,6144]{2,1,0:T(8,128)(2,1)}), bf16[8,16,6144]{2,1,0:T(8,128)(2,1)S(1)}, u32[]{:S(2)}, u32[]{:S(2)}) async-start(bf16[8,16,6144]{2,1,0:T(8,128)(2,1)} %get-tuple-element.7), calls=%async_computation.5 | async-start | bytes 3145728 | tf_op jit(solution)/shard_map/all_to_all | solution.py:45
  100.8 0.0 collective-permute-done.4.g1
  100.8 16.7 %all-to-all-done.5.x = bf16[8,16,6144]{2,1,0:T(8,128)(2,1)S(1)} async-done(((bf16[8,16,6144]{2,1,0:T(8,128)(2,1)}), bf16[8,16,6144]{2,1,0:T(8,128)(2,1)S(1)}, u32[]{:S(2)}, u32[]{:S(2)}) %all-to-all-start.5) | async-done | bytes 1572896 | tf_op jit(solution)/shard_map/all_to_all | solution.py:45
  117.5 1.9 %copy-done = bf16[6144,256]{1,0:T(8,128)(2,1)S(1)} copy-done((bf16[6144,256]{1,0:T(8,128)(2,1)S(1)}, bf16[6144,256]{1,0:T(8,128)(2,1)}, u32[]{:S(2)}) %copy-start) | copy-done | bytes 3145752
  119.4 1.9 %copy-done.1 = bf16[6144,256]{1,0:T(8,128)(2,1)S(1)} copy-done((bf16[6144,256]{1,0:T(8,128)(2,1)S(1)}, bf16[6144,256]{1,0:T(8,128)(2,1)}, u32[]{:S(2)}) %copy-start.1) | copy-done | bytes 3145752
  121.3 1.9 %copy-done.2 = bf16[256,6144]{1,0:T(8,128)(2,1)S(1)} copy-done((bf16[256,6144]{1,0:T(8,128)(2,1)S(1)}, bf16[256,6144]{1,0:T(8,128)(2,1)}, u32[]{:S(2)}) %copy-start.2) | copy-done | bytes 3145752
  123.2 13.0 %shard_map.142 = bf16[8,16,6144]{2,1,0:T(8,128)(2,1)S(1)} custom-call(s32[6]{0:T(128)S(1)} %stack.27.info, bf16[8,16,6144]{2,1,0:T(8,128)(2,1)S(1)} %all-to-all-done.5.x, s32[8,256]{1,0:T(8,128)S(1)} %pad.8.ids, bf16[8,6144]{1,0:T(8,128)(2,1)S(1)} %pad.9.router, bf16[6144,256]{1,0:T(8,128)(2,1)S(1)} %copy-done, bf16[6144,256]{1,0:T(8,128)(2,1)} %collective-permute-done.4.g1, ...), custom_call_target="tpu_custom_call" | custom-call | flops 2415919104 | bytes 23068672 | tf_op jit(solution)/shard_map/pallas_call | solution.py:328
  136.2 20.4 %all_to_all.41.parts = bf16[8,16,6144]{2,1,0:T(8,128)(2,1)S(1)} all-to-all(bf16[8,16,6144]{2,1,0:T(8,128)(2,1)S(1)} %shard_map.142), channel_id=1, replica_groups=mesh['dp'=2,'ctx'=16,'exp'=8] {'exp'}, dimensions={0} | all-to-all | bytes 3145728 | tf_op jit(solution)/shard_map/all_to_all | solution.py:45
  156.6 0.2 shard_map.143
  156.8 12.2 %all_to_all.42.parts = bf16[8,2,6144]{2,1,0:T(2,128)(2,1)S(1)} all-to-all(bf16[8,2,6144]{2,1,0:T(2,128)(2,1)S(1)} %shard_map.143), channel_id=1, replica_groups={{0,16,32,48,64,80,96,112},{8,24,40,56,72,88,104,120},{1,17,33,49,65,81,..., dimensions={0} | all-to-all | bytes 393216 | tf_op jit(solution)/shard_map/all_to_all | solution.py:41
  169.0 0.8 shard_map.144
  (22 shorter events, 0.1 us)
Async XLA Ops:
  0.0 22.6 %collective-permute-start = (bf16[4096,128]{1,0:T(8,128)(2,1)}, bf16[4096,128]{1,0:T(8,128)(2,1)S(1)}, u32[]{:S(2)}, u32[]{:S(2)}) collective-permute-start(bf16[4096,128]{1,0:T(8,128)(2,1)} %k0.1), channel_id=1, source_target_pairs={{0,8},{8,0},{16,24},{24,16},{32,40},{40,32},{48,56},{56,48},{64,72... | collective-permute-start | bytes 3145736 | tf_op jit(solution)/shard_map/ppermute | solution.py:49
  0.0 22.6 %collective-permute-start.1 = (bf16[4096,128]{1,0:T(8,128)(2,1)}, bf16[4096,128]{1,0:T(8,128)(2,1)S(1)}, u32[]{:S(2)}, u32[]{:S(2)}) collective-permute-start(bf16[4096,128]{1,0:T(8,128)(2,1)} %v0.1), channel_id=1, source_target_pairs={{0,8},{8,0},{16,24},{24,16},{32,40},{40,32},{48,56},{56,48},{64,72... | collective-permute-start | bytes 3145736 | tf_op jit(solution)/shard_map/ppermute | solution.py:49
  0.5 0.7 copy-start.4
  1.2 0.7 copy-start.5
  2.7 19.8 %all-to-all-start = ((bf16[8,112,128]{2,1,0:T(8,128)(2,1)}), bf16[8,112,128]{2,1,0:T(8,128)(2,1)S(1)}, u32[]{:S(2)}, u32[]{:S(2)}) async-start(bf16[8,112,128]{2,1,0:T(8,128)(2,1)} %shard_map.136), calls=%async_computation | async-start | bytes 458752 | tf_op jit(solution)/shard_map/all_to_all | solution.py:41
  12.6 1.3 collective-permute-start.2
  12.6 88.2 %collective-permute-start.4 = (bf16[6144,256]{1,0:T(8,128)(2,1)}, bf16[6144,256]{1,0:T(8,128)(2,1)}, u32[]{:S(2)}, u32[]{:S(2)}) collective-permute-start(bf16[6144,256]{1,0:T(8,128)(2,1)} %g0.1), channel_id=1, source_target_pairs={{0,8},{8,0},{16,24},{24,16},{32,40},{40,32},{48,56},{56,48},{64,72... | collective-permute-start | bytes 9437192 | tf_op jit(solution)/shard_map/ppermute | solution.py:49
  13.1 87.7 %collective-permute-start.5 = (bf16[6144,256]{1,0:T(8,128)(2,1)}, bf16[6144,256]{1,0:T(8,128)(2,1)}, u32[]{:S(2)}, u32[]{:S(2)}) collective-permute-start(bf16[6144,256]{1,0:T(8,128)(2,1)} %u0.1), channel_id=1, source_target_pairs={{0,8},{8,0},{16,24},{24,16},{32,40},{40,32},{48,56},{56,48},{64,72... | collective-permute-start | bytes 9437192 | tf_op jit(solution)/shard_map/ppermute | solution.py:49
  13.9 86.9 %collective-permute-start.6 = (bf16[256,6144]{1,0:T(8,128)(2,1)}, bf16[256,6144]{1,0:T(8,128)(2,1)}, u32[]{:S(2)}, u32[]{:S(2)}) collective-permute-start(bf16[256,6144]{1,0:T(8,128)(2,1)} %d0.1), channel_id=1, source_target_pairs={{0,8},{8,0},{16,24},{24,16},{32,40},{40,32},{48,56},{56,48},{64,72... | collective-permute-start | bytes 9437192 | tf_op jit(solution)/shard_map/ppermute | solution.py:49
  22.6 1.0 copy-start.8
  23.6 1.2 copy-start.6
  24.8 1.2 copy-start.7
  26.0 1.2 copy-start.9
  27.2 14.4 %copy-start.3 = (bf16[768,384]{1,0:T(8,128)(2,1)S(1)}, bf16[768,384]{1,0:T(8,128)(2,1)}, u32[]{:S(2)}) copy-start(bf16[768,384]{1,0:T(8,128)(2,1)} %own.1) | copy-start | bytes 1769476
  38.2 47.2 %copy-start.11 = (bf16[6144]{0:T(1024)(128)(2,1)S(1)}, bf16[6144]{0:T(1024)(128)(2,1)}, u32[]{:S(2)}) copy-start(bf16[6144]{0:T(1024)(128)(2,1)} %param.22) | copy-start | bytes 36868
  38.2 13.5 %all-to-all-start.1 = ((bf16[8,112,128]{2,1,0:T(8,128)(2,1)}), bf16[8,112,128]{2,1,0:T(8,128)(2,1)S(1)}, u32[]{:S(2)}, u32[]{:S(2)}) async-start(bf16[8,112,128]{2,1,0:T(8,128)(2,1)} %shard_map.137), calls=%async_computation.1 | async-start | bytes 458752 | tf_op jit(solution)/shard_map/all_to_all | solution.py:41
  41.7 14.5 %collective-permute-start.3 = (bf16[768,384]{1,0:T(8,128)(2,1)S(1)}, bf16[768,384]{1,0:T(8,128)(2,1)S(1)}, u32[]{:S(2)}, u32[]{:S(2)}) collective-permute-start(bf16[768,384]{1,0:T(8,128)(2,1)S(1)} %copy-done.3), channel_id=1, source_target_pairs={{0,8},{8,0},{16,24},{24,16},{32,40},{40,32},{48,56},{56,48},{64,72... | collective-permute-start | bytes 1769480 | tf_op jit(solution)/shard_map/ppermute | solution.py:49
  52.7 13.1 %all-to-all-start.2 = ((bf16[8,16,768]{2,1,0:T(8,128)(2,1)}), bf16[8,16,768]{2,1,0:T(8,128)(2,1)S(1)}, u32[]{:S(2)}, u32[]{:S(2)}) async-start(bf16[8,16,768]{2,1,0:T(8,128)(2,1)} %shard_map.138), calls=%async_computation.2 | async-start | bytes 393216 | tf_op jit(solution)/shard_map/all_to_all | solution.py:41
  56.1 44.6 %copy-start.12 = (s32[256,2]{0,1:T(2,128)S(1)}, s32[256,2]{0,1:T(2,128)}, u32[]{:S(2)}) copy-start(s32[256,2]{0,1:T(2,128)} %param.24) | copy-start | bytes 6148
  56.2 44.6 %copy-start.10 = (bf16[6144,4]{0,1:T(4,128)(2,1)S(1)}, bf16[6144,4]{0,1:T(4,128)(2,1)}, u32[]{:S(2)}) copy-start(bf16[6144,4]{0,1:T(4,128)(2,1)} %param.23) | copy-start | bytes 147460
  82.0 13.1 %all-to-all-start.4 = ((bf16[8,16,768]{2,1,0:T(8,128)(2,1)}), bf16[8,16,768]{2,1,0:T(8,128)(2,1)S(1)}, u32[]{:S(2)}, u32[]{:S(2)}) async-start(bf16[8,16,768]{2,1,0:T(8,128)(2,1)} %shard_map.140), calls=%async_computation.4 | async-start | bytes 393216 | tf_op jit(solution)/shard_map/all_to_all | solution.py:41
  97.1 20.4 %all-to-all-start.5 = ((bf16[8,16,6144]{2,1,0:T(8,128)(2,1)}), bf16[8,16,6144]{2,1,0:T(8,128)(2,1)S(1)}, u32[]{:S(2)}, u32[]{:S(2)}) async-start(bf16[8,16,6144]{2,1,0:T(8,128)(2,1)} %get-tuple-element.7), calls=%async_computation.5 | async-start | bytes 3145728 | tf_op jit(solution)/shard_map/all_to_all | solution.py:45
  117.5 1.9 %copy-start = (bf16[6144,256]{1,0:T(8,128)(2,1)S(1)}, bf16[6144,256]{1,0:T(8,128)(2,1)}, u32[]{:S(2)}) copy-start(bf16[6144,256]{1,0:T(8,128)(2,1)} %g0.1) | copy-start | bytes 9437188
  119.4 1.9 %copy-start.1 = (bf16[6144,256]{1,0:T(8,128)(2,1)S(1)}, bf16[6144,256]{1,0:T(8,128)(2,1)}, u32[]{:S(2)}) copy-start(bf16[6144,256]{1,0:T(8,128)(2,1)} %u0.1) | copy-start | bytes 9437188
  121.3 1.9 %copy-start.2 = (bf16[256,6144]{1,0:T(8,128)(2,1)S(1)}, bf16[256,6144]{1,0:T(8,128)(2,1)}, u32[]{:S(2)}) copy-start(bf16[256,6144]{1,0:T(8,128)(2,1)} %d0.1) | copy-start | bytes 9437188

commit v2 on v1

--- a/solution.py
+++ b/solution.py
@@ -23,7 +23,6 @@
 ROWS = NZ * BLOCK_ROWS
 Q_BLOCK = 256
 CHUNK = 4096
-MASKED_CHUNK = 1024
 MESSAGE_ROWS = BLOCK_ROWS + 16
 COLS = 768
 HALF = 384
@@ -52,6 +51,10 @@
 VMEM = pl.BlockSpec(memory_space=pltpu.VMEM)
 SMEM = pl.BlockSpec(memory_space=pltpu.SMEM)
 ANY = pl.BlockSpec(memory_space=pl.ANY)
+
+
+def in_hbm(x):
+    return pltpu.with_memory_space_constraint(x, pltpu.HBM)
 
 
 def call(kernel, shape, *args, specs=None, dtype=BF16, limit=32, flops=1 << 20, scratch=()):
@@ -90,14 +93,41 @@
     return first, second, rest - second
 
 
+def prepare_kernel(v0, v1, k1, values, keys, sem):
+    copy = pltpu.make_async_copy(k1, keys, sem)
+    copy.start()
+    for part, rows in enumerate((v0, v1)):
+        values[part, :HEAD_DIM, :] = rows[...].T
+        values[part, HEAD_DIM:, :] = jnp.ones((16, CHUNK), BF16)
+    copy.wait()
+
+
+def prepare(v0, v1, k1):
+    return pl.pallas_call(
+        prepare_kernel,
+        out_shape=(
+            pltpu.HBM((2, HEAD_DIM + 16, CHUNK), BF16),
+            pltpu.HBM((CHUNK, HEAD_DIM), BF16),
+        ),
+        in_specs=[VMEM, VMEM, ANY],
+        out_specs=(VMEM, ANY),
+        scratch_shapes=[pltpu.SemaphoreType.DMA],
+        compiler_params=pltpu.CompilerParams(vmem_limit_bytes=16 << 20),
+        cost_estimate=pl.CostEstimate(flops=0, bytes_accessed=6 << 20, transcendentals=0),
+    )(v0, v1, k1)
+
+
 def attention_kernel(
-    info, first, k0, v0, k1, v1, sk, sv, out, q, keys, values, peak, carried, sems
+    info, first, k0, k1, turned, sk, sv, out, q, keys, values, peak, carried, sems
 ):
     copies = []
-    for i, (source, target) in enumerate(((k0, keys), (v0, values), (k1, keys), (v1, values))):
-        place = pl.ds(i // 2 * CHUNK, CHUNK)
-        copies.append(pltpu.make_async_copy(source, target.at[place, :], sems.at[i]))
-        copies[i].start()
+    for part, source in enumerate((k0, k1)):
+        copies.append(pltpu.make_async_copy(source, keys.at[part], sems.at[2 * part]))
+        copies.append(
+            pltpu.make_async_copy(turned.at[part], values.at[part], sems.at[2 * part + 1])
+        )
+    for copy in copies:
+        copy.start()
     q[...] = first[:, :BLOCK_ROWS, :].reshape(ROWS, HEAD_DIM)
     blocks = ROWS // Q_BLOCK
 
@@ -109,12 +139,9 @@
             rows, q[columns(b), :], (((1,), (1,)), ((), ())), preferred_element_type=F32
         )
 
-    def with_ones(rows):
-        return jnp.concatenate([rows.T, jnp.ones((16, rows.shape[0]), BF16)], axis=0)
-
     core = info[2]
     span_rows = 2 * BLOCK_TOKENS
-    span_values = with_ones(sv[...])
+    span_values = jnp.concatenate([sv[...].T, jnp.ones((16, span_rows), BF16)], axis=0)
     for b in range(blocks):
         row = lax.broadcasted_iota(jnp.int32, (span_rows, Q_BLOCK), 0)
         col = lax.broadcasted_iota(jnp.int32, (span_rows, Q_BLOCK), 1) + b * Q_BLOCK
@@ -133,43 +160,57 @@
         w = jnp.exp2((s - top) * EXP2_SCALE).astype(BF16)
         return w, jnp.exp2((before - top) * EXP2_SCALE)
 
-    def gather(b, w, factor, rows):
-        carried[:, columns(b)] = carried[:, columns(b)] * factor + jnp.dot(
-            rows, w, preferred_element_type=F32
-        )
-
-    for part in range(2):
-        valid = info[part]
-        copies[2 * part].wait()
-        copies[2 * part + 1].wait()
-
-        @pl.when(valid == CHUNK)
-        def _(part=part):
-            place = slice(part * CHUNK, (part + 1) * CHUNK)
-            key_rows = keys[place, :]
-            value_rows = with_ones(values[place, :])
-            s = scores_of(key_rows, 0)
-            earlier = None
-            for b in range(blocks):
-                later = scores_of(key_rows, b + 1) if b + 1 < blocks else None
-                current = soften(s, b)
-                if earlier is not None:
-                    gather(b - 1, *earlier, value_rows)
-                earlier, s = current, later
-            gather(blocks - 1, *earlier, value_rows)
-
-        @pl.when(valid < CHUNK)
-        def _(part=part, valid=valid):
-            @pl.loop(0, (valid + MASKED_CHUNK - 1) // MASKED_CHUNK)
-            def _(j):
-                start = pl.multiple_of(part * CHUNK + j * MASKED_CHUNK, MASKED_CHUNK)
-                key_rows = keys[pl.ds(start, MASKED_CHUNK), :]
-                value_rows = with_ones(values[pl.ds(start, MASKED_CHUNK), :])
-                row = lax.broadcasted_iota(jnp.int32, (MASKED_CHUNK, Q_BLOCK), 0)
-                for b in range(blocks):
-                    s = scores_of(key_rows, b)
-                    s = jnp.where(row + j * MASKED_CHUNK < valid, s, MASKED)
-                    gather(b, *soften(s, b), value_rows)
+    def run(parts, count, valid=None):
+        items = [(part, b) for part in parts for b in range(blocks)]
+
+        def scores(item):
+            s = scores_of(keys[item[0], :count, :], item[1])
+            if valid is not None:
+                row = lax.broadcasted_iota(jnp.int32, (count, Q_BLOCK), 0)
+                s = jnp.where(row < valid, s, MASKED)
+            return s
+
+        def gather(item, w, factor):
+            part, b = item
+            carried[:, columns(b)] = carried[:, columns(b)] * factor + jnp.dot(
+                values[part, :, :count], w, preferred_element_type=F32
+            )
+
+        s = scores(items[0])
+        earlier = None
+        for i, item in enumerate(items):
+            later = scores(items[i + 1]) if i + 1 < len(items) else None
+            current = soften(s, item[1])
+            if earlier is not None:
+                gather(items[i - 1], *earlier)
+            earlier, s = current, later
+        gather(items[-1], *earlier)
+
+    for copy in copies:
+        copy.wait()
+    everything = (info[0] == CHUNK) & (info[1] == CHUNK)
+
+    @pl.when(everything)
+    def _():
+        run((0, 1), CHUNK)
+
+    @pl.when(jnp.logical_not(everything))
+    def _():
+        @pl.loop(0, 2)
+        def _(part):
+            valid = info[part]
+
+            @pl.when(valid == CHUNK)
+            def _():
+                run((part,), CHUNK)
+
+            @pl.when((valid < CHUNK) & (valid > CHUNK // 2))
+            def _():
+                run((part,), CHUNK, valid)
+
+            @pl.when((valid <= CHUNK // 2) & (valid > 0))
+            def _():
+                run((part,), CHUNK // 2, valid)
 
     rows = carried[:HEAD_DIM, :].T.astype(BF16)
     out[:, :BLOCK_ROWS, :] = rows.reshape(NZ, BLOCK_ROWS, HEAD_DIM)
@@ -179,8 +220,8 @@
     for i, term in enumerate(terms):
         stats = jnp.where(row == i, term, stats)
     for z in range(NZ):
-        turned = stats if z == 0 else pltpu.roll(stats, ROWS - z * BLOCK_ROWS, 1)
-        out[z, BLOCK_ROWS:, :] = turned[:, :HEAD_DIM].astype(BF16)
+        shifted = stats if z == 0 else pltpu.roll(stats, ROWS - z * BLOCK_ROWS, 1)
+        out[z, BLOCK_ROWS:, :] = shifted[:, :HEAD_DIM].astype(BF16)
 
 
 def combine_kernel(message, out):
@@ -257,94 +298,84 @@
         own[:, place] = jnp.dot(pick, mid, preferred_element_type=F32).astype(BF16)
 
 
-MOE_STEPS = 8
-MOE_TILE = D // MOE_STEPS
-
-
-def moe_kernel(
-    info, x, ids, router, g0, g1, u0, u1, d0, d1, out, gate, up, logits, hidden, share
-):
-    step = pl.program_id(0)
-    units = g0.shape[1]
-
-    @pl.when(step == 0)
-    def _():
-        gate[...] = jnp.zeros(gate.shape, F32)
-        up[...] = jnp.zeros(up.shape, F32)
-        logits[...] = jnp.zeros(logits.shape, F32)
-
-    @pl.when(step < MOE_STEPS)
-    def _():
-        place = pl.ds(pl.multiple_of(step * MOE_TILE, MOE_TILE), MOE_TILE)
-        rows = x[:, :, place].reshape(128, MOE_TILE)
-        for i, (g, u) in enumerate(((g0, u0), (g1, u1))):
-            side = slice(i * units, (i + 1) * units)
-            gate[:, side] += jnp.dot(rows, g[...], preferred_element_type=F32)
-            up[:, side] += jnp.dot(rows, u[...], preferred_element_type=F32)
-        logits[...] += lax.dot_general(
-            rows, router[:, place], (((1,), (1,)), ((), ())), preferred_element_type=F32
-        )
-
-    @pl.when(step == MOE_STEPS - 1)
-    def _():
-        g = gate[...]
-        hidden[...] = (g / (1.0 + jnp.exp(-g)) * up[...]).astype(BF16)
-        core, expert = info[2], info[5]
-        r = lax.broadcasted_iota(jnp.int32, (128, SPAN), 0)
-        u = lax.broadcasted_iota(jnp.int32, (128, SPAN), 1)
-        token = (r % 16 // FINE * 2 + core) * BLOCK_TOKENS + r // 16 * FINE + r % FINE
-        leading, trailing = ids[0:1, :], ids[1:2, :]
-        chosen = (leading == expert) | (trailing == expert)
-        other = jnp.where(leading == expert, trailing, leading)
-        earlier = jnp.sum(jnp.where(chosen & (u < token), 1.0, 0.0), axis=1, keepdims=True)
-        mine = jnp.sum(jnp.where(chosen & (u == token), 1.0, 0.0), axis=1, keepdims=True)
-        other_id = jnp.sum(jnp.where(u == token, other.astype(F32), 0.0), axis=1, keepdims=True)
-        lane = lax.broadcasted_iota(jnp.int32, logits.shape, 1)
-        values = logits[...]
-        own_logit = jnp.sum(jnp.where(lane == expert, values, 0.0), axis=1, keepdims=True)
-        other_logit = jnp.sum(
-            jnp.where(lane.astype(F32) == other_id, values, 0.0), axis=1, keepdims=True
-        )
-        active = (mine > 0.5) & (earlier < CAP - 0.5)
-        share[...] = jnp.broadcast_to(
-            jnp.where(active, 1.0 / (1.0 + jnp.exp(other_logit - own_logit)), 0.0), share.shape
-        )
-
-    @pl.when(step >= MOE_STEPS)
-    def _():
-        total = jnp.dot(hidden[:, :units], d0[...], preferred_element_type=F32)
-        total = total + jnp.dot(hidden[:, units:], d1[...], preferred_element_type=F32)
-        out[...] = (total * share[:, :1]).astype(BF16).reshape(NE, 16, MOE_TILE)
-
-
-def experts(info, x, ids, router, g0, g1, u0, u1, d0, d1):
-    units = g0.shape[1]
-    wide = pl.BlockSpec((MOE_TILE, units), lambda i: (jnp.minimum(i, MOE_STEPS - 1), 0))
-    down = pl.BlockSpec((units, MOE_TILE), lambda i: (0, jnp.maximum(i - MOE_STEPS, 0)))
-
-    def whole(a):
-        return pl.BlockSpec(a.shape, lambda i: (0,) * a.ndim)
-
-    return pl.pallas_call(
+MOE_PIECES = 4
+MOE_TILE = D // MOE_PIECES
+
+
+def moe_kernel(info, x, ids, router, *refs):
+    sources, out, held, sems = refs[:6], refs[6], refs[7:13], refs[13]
+    units = sources[0].shape[1]
+    copies = []
+    for k in range(2 * MOE_PIECES):
+        place = pl.ds(k % MOE_PIECES * MOE_TILE, MOE_TILE)
+        group = range(4) if k < MOE_PIECES else range(4, 6)
+        copies.append([])
+        for i in group:
+            at = (place, slice(None)) if i < 4 else (slice(None), place)
+            copy = pltpu.make_async_copy(sources[i].at[at], held[i].at[at], sems.at[k, i % 4])
+            copy.start()
+            copies[k].append(copy)
+
+    core, expert = info[2], info[5]
+    rows = x[...].reshape(128, D)
+    logits = lax.dot_general(
+        rows, router[...], (((1,), (1,)), ((), ())), preferred_element_type=F32
+    )
+    r = lax.broadcasted_iota(jnp.int32, (128, SPAN), 0)
+    u = lax.broadcasted_iota(jnp.int32, (128, SPAN), 1)
+    token = (r % 16 // FINE * 2 + core) * BLOCK_TOKENS + r // 16 * FINE + r % FINE
+    leading, trailing = ids[0:1, :], ids[1:2, :]
+    chosen = (leading == expert) | (trailing == expert)
+    other = jnp.where(leading == expert, trailing, leading)
+    earlier = jnp.sum(jnp.where(chosen & (u < token), 1.0, 0.0), axis=1, keepdims=True)
+    mine = jnp.sum(jnp.where(chosen & (u == token), 1.0, 0.0), axis=1, keepdims=True)
+    other_id = jnp.sum(jnp.where(u == token, other.astype(F32), 0.0), axis=1, keepdims=True)
+    lane = lax.broadcasted_iota(jnp.int32, logits.shape, 1)
+    own_logit = jnp.sum(jnp.where(lane == expert, logits, 0.0), axis=1, keepdims=True)
+    other_logit = jnp.sum(
+        jnp.where(lane.astype(F32) == other_id, logits, 0.0), axis=1, keepdims=True
+    )
+    active = (mine > 0.5) & (earlier < CAP - 0.5)
+    share = jnp.where(active, 1.0 / (1.0 + jnp.exp(other_logit - own_logit)), 0.0)
+
+    sums = [jnp.zeros((128, units), F32)] * 4
+    for k in range(MOE_PIECES):
+        for copy in copies[k]:
+            copy.wait()
+        place = slice(k * MOE_TILE, (k + 1) * MOE_TILE)
+        part = x[:, :, place].reshape(128, MOE_TILE)
+        sums = [
+            sums[i] + jnp.dot(part, held[i][place, :], preferred_element_type=F32) for i in range(4)
+        ]
+    hidden = [
+        (sums[i] / (1.0 + jnp.exp(-sums[i])) * sums[i + 2]).astype(BF16) for i in range(2)
+    ]
+    for k in range(MOE_PIECES):
+        for copy in copies[MOE_PIECES + k]:
+            copy.wait()
+        place = slice(k * MOE_TILE, (k + 1) * MOE_TILE)
+        total = jnp.dot(hidden[0], held[4][:, place], preferred_element_type=F32)
+        total = total + jnp.dot(hidden[1], held[5][:, place], preferred_element_type=F32)
+        out[:, :, place] = (total * share).astype(BF16).reshape(NE, 16, MOE_TILE)
+
+
+def experts(info, x, ids, router, *weights):
+    units = weights[0].shape[1]
+    return call(
         moe_kernel,
-        grid=(2 * MOE_STEPS,),
-        out_shape=jax.ShapeDtypeStruct((NE, 16, D), BF16),
-        in_specs=[SMEM, whole(x), whole(ids), whole(router)] + [wide] * 4 + [down] * 2,
-        out_specs=pl.BlockSpec(
-            (NE, 16, MOE_TILE), lambda i: (0, 0, jnp.maximum(i - MOE_STEPS, 0))
-        ),
-        scratch_shapes=[
-            pltpu.VMEM((128, 2 * units), F32),
-            pltpu.VMEM((128, 2 * units), F32),
-            pltpu.VMEM((128, 8), F32),
-            pltpu.VMEM((128, 2 * units), BF16),
-            pltpu.VMEM((128, 128), F32),
-        ],
-        compiler_params=pltpu.CompilerParams(vmem_limit_bytes=24 << 20),
-        cost_estimate=pl.CostEstimate(
-            flops=6 * 128 * D * 2 * units, bytes_accessed=22 << 20, transcendentals=128 * 512
-        ),
-    )(info, x, ids, router, g0, g1, u0, u1, d0, d1)
+        (NE, 16, D),
+        info,
+        x,
+        ids,
+        router,
+        *[in_hbm(w) for w in weights],
+        specs=[SMEM] + [VMEM] * 3 + [ANY] * 6,
+        limit=40,
+        flops=6 * 128 * D * 512,
+        scratch=[pltpu.VMEM((D, units), BF16)] * 4
+        + [pltpu.VMEM((units, D), BF16)] * 2
+        + [pltpu.SemaphoreType.DMA((2 * MOE_PIECES, 4))],
+    )
 
 
 def sum_kernel(parts, out):
@@ -393,7 +424,7 @@
     other_down = sibling(down_weight)
 
     first = exchange_z(
-        call(first_message_kernel, (NZ, MESSAGE_ROWS, HEAD_DIM), queries, residual)
+        call(first_message_kernel, (NZ, MESSAGE_ROWS, HEAD_DIM), in_hbm(queries), in_hbm(residual))
     )
 
     def valid(index):
@@ -413,25 +444,25 @@
             z_index // 2,
         ]
     ).astype(jnp.int32)
+    prepared_values, prepared_keys = prepare(in_hbm(cache_values), other_values, other_keys)
     second = exchange_z(
         call(
             attention_kernel,
             (NZ, MESSAGE_ROWS, HEAD_DIM),
             info,
             first,
-            cache_keys,
-            cache_values,
-            other_keys,
-            other_values,
+            in_hbm(cache_keys),
+            in_hbm(prepared_keys),
+            in_hbm(prepared_values),
             span_both[:, :HEAD_DIM],
             span_both[:, HEAD_DIM:],
-            specs=[SMEM, VMEM, ANY, ANY, ANY, ANY, VMEM, VMEM],
+            specs=[SMEM, VMEM, ANY, ANY, ANY, VMEM, VMEM],
             limit=48,
             flops=4 * ROWS * 2 * CHUNK * HEAD_DIM,
             scratch=[
                 pltpu.VMEM((ROWS, HEAD_DIM), BF16),
-                pltpu.VMEM((2 * CHUNK, HEAD_DIM), BF16),
-                pltpu.VMEM((2 * CHUNK, HEAD_DIM), BF16),
+                pltpu.VMEM((2, CHUNK, HEAD_DIM), BF16),
+                pltpu.VMEM((2, HEAD_DIM + 16, CHUNK), BF16),
                 pltpu.VMEM((8, ROWS), F32),
                 pltpu.VMEM((HEAD_DIM + 16, ROWS), F32),
                 pltpu.SemaphoreType.DMA((4,)),
@@ -461,16 +492,14 @@
         out_specs=(VMEM, VMEM),
         compiler_params=pltpu.CompilerParams(vmem_limit_bytes=16 << 20),
         cost_estimate=pl.CostEstimate(flops=1 << 20, bytes_accessed=2 << 20, transcendentals=0),
-    )(info, fifth, norm_gain.reshape(1, D))
+    )(info, fifth, in_hbm(norm_gain.reshape(1, D)))
     tokens = exchange_exp(normed)
 
-    ids = jnp.pad(expert_ids.T, ((0, 8 - TOPK), (0, 0)))
-    router = jnp.pad(router_weight.T, ((0, 8 - EXPERTS), (0, 0)))
     result = experts(
         info,
         tokens,
-        ids,
-        router,
+        in_hbm(expert_ids.T),
+        in_hbm(router_weight.T),
         gate_weight,
         other_gate,
         up_weight,

time: 171 us -> 157 us (0.918)
  local copies, waits for them, and re-layouts: 13.3 us -> 2.1 us
  waiting for transfers between devices: 54.1 us -> 49.5 us
    unnamed x27 -> x5, local copies, waits for them, and re-layouts: 12.5 us -> 0.7 us
    pallas_call x7 -> x8, Pallas kernels: 15.6 us -> 26.3 us  [call(): pl.pallas_call(kernel, out_shape=jax.ShapeDtypeStruct(shape, dtype), in_s...]
    pallas_call x1, Pallas kernels: 13 us -> 3.64 us  [prepare(): pl.pallas_call(prepare_kernel, out_shape=(pltpu.HBM((2, HEAD_DIM + 16, CH...]
    all_to_all x4, waiting for transfers between devices: 37.4 us -> 32.9 us  [exchange_z(): lax.all_to_all(blocks, 'ctx', 0, 0, axis_index_groups=Z_GROUPS, tiled=True)]
  transfers between devices with their start and end apart: 12 -> 12, of which waited for: 5 -> 5; matrix products, arithmetic and copies ran while one was open for 1% -> 1% of each run, Pallas kernels for 10% -> 14%
where the time goes in v2:
time: 157 us; the launch traced here: 155 us
  waiting for transfers between devices  49.5 us (32%)
  blocking collectives  46.7 us (30%)
  Pallas kernels  32.1 us (20%)
  starting transfers between devices  24.2 us (15%)
  local copies, waits for them, and re-layouts  2.1 us (1%)
    all_to_all x2, blocking collectives, exchange_exp(): return lax.all_to_all(blocks, 'exp', 0, 0, tiled=True)  34.5 us
    all_to_all x4, waiting for transfers between devices, exchange_z(): lax.all_to_all(blocks, 'ctx', 0, 0, axis_index_groups=Z_GROUPS, tiled=True)  32.9 us
    pallas_call x8, Pallas kernels, call(): pl.pallas_call(kernel, out_shape=jax.ShapeDtypeStruct(shape, dtype), in_s...  26.3 us
    all_to_all x4, starting transfers between devices, exchange_z(): lax.all_to_all(blocks, 'ctx', 0, 0, axis_index_groups=Z_GROUPS, tiled=True)  18.9 us
    all_to_all x1, waiting for transfers between devices, exchange_exp(): return lax.all_to_all(blocks, 'exp', 0, 0, tiled=True)  16.6 us
    all_to_all x1, blocking collectives, exchange_z(): lax.all_to_all(blocks, 'ctx', 0, 0, axis_index_groups=Z_GROUPS, tiled=True)  12.2 us
    pallas_call x1, Pallas kernels, prepare(): pl.pallas_call(prepare_kernel, out_shape=(pltpu.HBM((2, HEAD_DIM + 16, CH...  3.64 us
    all_to_all x1, starting transfers between devices, exchange_exp(): return lax.all_to_all(blocks, 'exp', 0, 0, tiled=True)  3.58 us
  transfers between devices with their start and end apart: 12, of which 5 were waited for; matrix products, arithmetic and copies ran while one was open for 1% of the time, Pallas kernels for 14%

profile of v2, /device:TPU:2, one launch (start us, length us, event | category | flops | bytes accessed | tf_op | source)
XLA Modules:
  0.0 155.4 jit_solution(653817302984867022)
XLA Ops:
  0.0 0.0 collective-permute-start.1
  0.0 0.5 collective-permute-start
  0.5 1.5 shard_map.136
  2.0 8.5 %all-to-all-start = ((bf16[8,112,128]{2,1,0:T(8,128)(2,1)}), bf16[8,112,128]{2,1,0:T(8,128)(2,1)S(1)}, u32[]{:S(2)}, u32[]{:S(2)}) async-start(bf16[8,112,128]{2,1,0:T(8,128)(2,1)} %shard_map.136), calls=%async_computation | async-start | bytes 458752 | tf_op jit(solution)/shard_map/all_to_all | solution.py:40
  10.5 0.7 constant_dynamic-update-slice_fusion.1
  11.2 0.7 constant_dynamic-update-slice_fusion
  11.9 0.0 collective-permute-start.2
  11.9 0.5 collective-permute-start.4
  12.4 0.0 collective-permute-start.5
  13.1 0.1 stack.27.info
  13.1 0.0 collective-permute-done.2
  13.1 0.6 collective-permute-start.6
  13.7 0.0 collective-permute-done.1.k1
  13.7 0.0 collective-permute-done.v1
  13.7 3.6 %shard_map.137 = (bf16[2,144,4096]{2,1,0:T(8,128)(2,1)}, bf16[4096,128]{1,0:T(8,128)(2,1)}) custom-call(bf16[4096,128]{1,0:T(8,128)(2,1)} %v0.1, bf16[4096,128]{1,0:T(8,128)(2,1)S(1)} %collective-permute-done.v1, bf16[4096,128]{1,0:T(8,128)(2,1)S(1)} %collective-permute-done.1.k1), custom_call_target="tpu_custom_call" | custom-call | bytes 6291456 | tf_op jit(solution)/shard_map/pallas_call | solution.py:106
  17.4 4.5 %all-to-all-done.first.message = bf16[8,112,128]{2,1,0:T(8,128)(2,1)S(1)} async-done(((bf16[8,112,128]{2,1,0:T(8,128)(2,1)}), bf16[8,112,128]{2,1,0:T(8,128)(2,1)S(1)}, u32[]{:S(2)}, u32[]{:S(2)}) %all-to-all-start) | async-done | bytes 229408 | tf_op jit(solution)/shard_map/all_to_all | solution.py:40
  21.8 0.0 copy-start
  21.8 11.7 %shard_map.138 = bf16[8,112,128]{2,1,0:T(8,128)(2,1)} custom-call(s32[6]{0:T(128)S(1)} %stack.27.info, bf16[8,112,128]{2,1,0:T(8,128)(2,1)S(1)} %all-to-all-done.first.message, bf16[4096,128]{1,0:T(8,128)(2,1)} %k0.1, bf16[4096,128]{1,0:T(8,128)(2,1)} %get-tuple-element.9.k1, bf16[2,144,4096]{2,1,0:T(8,128)(2,1)} %get-tuple-element.10.turned, ...), custom_call_target="tpu_custom_call" | custom-call | flops 3221225472 | bytes 1048576 | tf_op jit(solution)/shard_map/pallas_call | solution.py:61
  33.5 0.0 copy-start.1
  33.5 3.4 %all-to-all-start.1 = ((bf16[8,112,128]{2,1,0:T(8,128)(2,1)}), bf16[8,112,128]{2,1,0:T(8,128)(2,1)S(1)}, u32[]{:S(2)}, u32[]{:S(2)}) async-start(bf16[8,112,128]{2,1,0:T(8,128)(2,1)} %shard_map.138), calls=%async_computation.1 | async-start | bytes 458752 | tf_op jit(solution)/shard_map/all_to_all | solution.py:40
  36.9 0.0 copy-done
  37.0 0.1 collective-permute-start.3
  37.1 9.9 %all-to-all-done.1.message = bf16[8,112,128]{2,1,0:T(8,128)(2,1)S(1)} async-done(((bf16[8,112,128]{2,1,0:T(8,128)(2,1)}), bf16[8,112,128]{2,1,0:T(8,128)(2,1)S(1)}, u32[]{:S(2)}, u32[]{:S(2)}) %all-to-all-start.1) | async-done | bytes 229408 | tf_op jit(solution)/shard_map/all_to_all | solution.py:40
  47.0 1.0 shard_map.139
  48.0 3.7 %all-to-all-start.2 = ((bf16[8,16,768]{2,1,0:T(8,128)(2,1)}), bf16[8,16,768]{2,1,0:T(8,128)(2,1)S(1)}, u32[]{:S(2)}, u32[]{:S(2)}) async-start(bf16[8,16,768]{2,1,0:T(8,128)(2,1)} %shard_map.139), calls=%async_computation.2 | async-start | bytes 393216 | tf_op jit(solution)/shard_map/all_to_all | solution.py:40
  51.7 0.0 collective-permute-done.3.other
  51.7 9.4 %all-to-all-done.2.x = bf16[8,16,768]{2,1,0:T(8,128)(2,1)S(1)} async-done(((bf16[8,16,768]{2,1,0:T(8,128)(2,1)}), bf16[8,16,768]{2,1,0:T(8,128)(2,1)S(1)}, u32[]{:S(2)}, u32[]{:S(2)}) %all-to-all-start.2) | async-done | bytes 196640 | tf_op jit(solution)/shard_map/all_to_all | solution.py:40
  61.1 1.0 shard_map.140
  62.1 14.3 %all_to_all.40.parts = bf16[8,16,768]{2,1,0:T(8,128)(2,1)S(1)} all-to-all(bf16[8,16,768]{2,1,0:T(8,128)(2,1)S(1)} %shard_map.140), channel_id=1, replica_groups=mesh['dp'=2,'ctx'=16,'exp'=8] {'exp'}, dimensions={0} | all-to-all | bytes 393216 | tf_op jit(solution)/shard_map/all_to_all | solution.py:44
  76.4 0.9 shard_map.141
  77.3 3.4 %all-to-all-start.4 = ((bf16[8,16,768]{2,1,0:T(8,128)(2,1)}), bf16[8,16,768]{2,1,0:T(8,128)(2,1)S(1)}, u32[]{:S(2)}, u32[]{:S(2)}) async-start(bf16[8,16,768]{2,1,0:T(8,128)(2,1)} %shard_map.141), calls=%async_computation.4 | async-start | bytes 393216 | tf_op jit(solution)/shard_map/all_to_all | solution.py:40
  80.7 0.0 copy-done.1
  80.7 0.6 reshape.3.gain
  81.3 9.1 %all-to-all-done.4.parts = bf16[8,16,768]{2,1,0:T(8,128)(2,1)S(1)} async-done(((bf16[8,16,768]{2,1,0:T(8,128)(2,1)}), bf16[8,16,768]{2,1,0:T(8,128)(2,1)S(1)}, u32[]{:S(2)}, u32[]{:S(2)}) %all-to-all-start.4) | async-done | bytes 196640 | tf_op jit(solution)/shard_map/all_to_all | solution.py:40
  90.4 2.2 %shard_map.142 = (bf16[8,16,6144]{2,1,0:T(8,128)(2,1)}, bf16[16,6144]{1,0:T(8,128)(2,1)S(1)}) custom-call(s32[6]{0:T(128)S(1)} %stack.27.info, bf16[8,16,768]{2,1,0:T(8,128)(2,1)S(1)} %all-to-all-done.4.parts, bf16[1,6144]{1,0:T(2,128)(2,1)} %reshape.3.gain), custom_call_target="tpu_custom_call" | custom-call | flops 1048576 | bytes 2097152 | tf_op jit(solution)/shard_map/pallas_call | solution.py:485
  92.6 3.6 %all-to-all-start.5 = ((bf16[8,16,6144]{2,1,0:T(8,128)(2,1)}), bf16[8,16,6144]{2,1,0:T(8,128)(2,1)S(1)}, u32[]{:S(2)}, u32[]{:S(2)}) async-start(bf16[8,16,6144]{2,1,0:T(8,128)(2,1)} %get-tuple-element.11), calls=%async_computation.5 | async-start | bytes 3145728 | tf_op jit(solution)/shard_map/all_to_all | solution.py:44
  96.2 0.0 collective-permute-done.4.refs_1_
  96.2 0.0 collective-permute-done.5.refs_3_
  96.2 0.0 collective-permute-done.6.refs_5_
  96.2 16.6 %all-to-all-done.5.x = bf16[8,16,6144]{2,1,0:T(8,128)(2,1)S(1)} async-done(((bf16[8,16,6144]{2,1,0:T(8,128)(2,1)}), bf16[8,16,6144]{2,1,0:T(8,128)(2,1)S(1)}, u32[]{:S(2)}, u32[]{:S(2)}) %all-to-all-start.5) | async-done | bytes 1572896 | tf_op jit(solution)/shard_map/all_to_all | solution.py:44
  112.8 9.2 %shard_map.143 = bf16[8,16,6144]{2,1,0:T(8,128)(2,1)S(1)} custom-call(s32[6]{0:T(128)S(1)} %stack.27.info, bf16[8,16,6144]{2,1,0:T(8,128)(2,1)S(1)} %all-to-all-done.5.x, s32[2,256]{1,0:T(2,128)} %bitcast.12, bf16[4,6144]{1,0:T(4,128)(2,1)} %bitcast.11, bf16[6144,256]{1,0:T(8,128)(2,1)} %refs_0_.1, bf16[6144,256]{1,0:T(8,128)(2,1)} %collective-permute-done.4.refs_1_, ...), custom_call_target="tpu_custom_call" | custom-call | flops 2415919104 | bytes 1048576 | tf_op jit(solution)/shard_map/pallas_call | solution.py:61
  122.0 20.2 %all_to_all.41.parts = bf16[8,16,6144]{2,1,0:T(8,128)(2,1)S(1)} all-to-all(bf16[8,16,6144]{2,1,0:T(8,128)(2,1)S(1)} %shard_map.143), channel_id=1, replica_groups=mesh['dp'=2,'ctx'=16,'exp'=8] {'exp'}, dimensions={0} | all-to-all | bytes 3145728 | tf_op jit(solution)/shard_map/all_to_all | solution.py:44
  142.3 0.2 shard_map.144
  142.5 12.2 %all_to_all.42.parts = bf16[8,2,6144]{2,1,0:T(2,128)(2,1)S(1)} all-to-all(bf16[8,2,6144]{2,1,0:T(2,128)(2,1)S(1)} %shard_map.144), channel_id=1, replica_groups={{0,16,32,48,64,80,96,112},{8,24,40,56,72,88,104,120},{1,17,33,49,65,81,..., dimensions={0} | all-to-all | bytes 393216 | tf_op jit(solution)/shard_map/all_to_all | solution.py:40
  154.7 0.8 shard_map.145
  (2 shorter events, 0.0 us)
Async XLA Ops:
  0.0 13.7 %collective-permute-start.1 = (bf16[4096,128]{1,0:T(8,128)(2,1)}, bf16[4096,128]{1,0:T(8,128)(2,1)S(1)}, u32[]{:S(2)}, u32[]{:S(2)}) collective-permute-start(bf16[4096,128]{1,0:T(8,128)(2,1)} %k0.1), channel_id=1, source_target_pairs={{0,8},{8,0},{16,24},{24,16},{32,40},{40,32},{48,56},{56,48},{64,72... | collective-permute-start | bytes 3145736 | tf_op jit(solution)/shard_map/ppermute | solution.py:48
  0.0 13.7 %collective-permute-start = (bf16[4096,128]{1,0:T(8,128)(2,1)}, bf16[4096,128]{1,0:T(8,128)(2,1)S(1)}, u32[]{:S(2)}, u32[]{:S(2)}) collective-permute-start(bf16[4096,128]{1,0:T(8,128)(2,1)} %v0.1), channel_id=1, source_target_pairs={{0,8},{8,0},{16,24},{24,16},{32,40},{40,32},{48,56},{56,48},{64,72... | collective-permute-start | bytes 3145736 | tf_op jit(solution)/shard_map/ppermute | solution.py:48
  2.0 19.8 %all-to-all-start = ((bf16[8,112,128]{2,1,0:T(8,128)(2,1)}), bf16[8,112,128]{2,1,0:T(8,128)(2,1)S(1)}, u32[]{:S(2)}, u32[]{:S(2)}) async-start(bf16[8,112,128]{2,1,0:T(8,128)(2,1)} %shard_map.136), calls=%async_computation | async-start | bytes 458752 | tf_op jit(solution)/shard_map/all_to_all | solution.py:40
  11.9 1.3 collective-permute-start.2
  11.9 84.3 %collective-permute-start.4 = (bf16[6144,256]{1,0:T(8,128)(2,1)}, bf16[6144,256]{1,0:T(8,128)(2,1)}, u32[]{:S(2)}, u32[]{:S(2)}) collective-permute-start(bf16[6144,256]{1,0:T(8,128)(2,1)} %refs_0_.1), channel_id=1, source_target_pairs={{0,8},{8,0},{16,24},{24,16},{32,40},{40,32},{48,56},{56,48},{64,72... | collective-permute-start | bytes 9437192 | tf_op jit(solution)/shard_map/ppermute | solution.py:48
  12.4 83.8 %collective-permute-start.5 = (bf16[6144,256]{1,0:T(8,128)(2,1)}, bf16[6144,256]{1,0:T(8,128)(2,1)}, u32[]{:S(2)}, u32[]{:S(2)}) collective-permute-start(bf16[6144,256]{1,0:T(8,128)(2,1)} %refs_2_.1), channel_id=1, source_target_pairs={{0,8},{8,0},{16,24},{24,16},{32,40},{40,32},{48,56},{56,48},{64,72... | collective-permute-start | bytes 9437192 | tf_op jit(solution)/shard_map/ppermute | solution.py:48
  13.1 83.0 %collective-permute-start.6 = (bf16[256,6144]{1,0:T(8,128)(2,1)}, bf16[256,6144]{1,0:T(8,128)(2,1)}, u32[]{:S(2)}, u32[]{:S(2)}) collective-permute-start(bf16[256,6144]{1,0:T(8,128)(2,1)} %refs_4_.1), channel_id=1, source_target_pairs={{0,8},{8,0},{16,24},{24,16},{32,40},{40,32},{48,56},{56,48},{64,72... | collective-permute-start | bytes 9437192 | tf_op jit(solution)/shard_map/ppermute | solution.py:48
  21.8 15.1 %copy-start = (bf16[768,384]{1,0:T(8,128)(2,1)S(1)}, bf16[768,384]{1,0:T(8,128)(2,1)}, u32[]{:S(2)}) copy-start(bf16[768,384]{1,0:T(8,128)(2,1)} %own.1) | copy-start | bytes 1769476
  33.5 47.2 %copy-start.1 = (bf16[6144]{0:T(1024)(128)(2,1)S(1)}, bf16[6144]{0:T(1024)(128)(2,1)}, u32[]{:S(2)}) copy-start(bf16[6144]{0:T(1024)(128)(2,1)} %param.22) | copy-start | bytes 36868
  33.5 13.5 %all-to-all-start.1 = ((bf16[8,112,128]{2,1,0:T(8,128)(2,1)}), bf16[8,112,128]{2,1,0:T(8,128)(2,1)S(1)}, u32[]{:S(2)}, u32[]{:S(2)}) async-start(bf16[8,112,128]{2,1,0:T(8,128)(2,1)} %shard_map.138), calls=%async_computation.1 | async-start | bytes 458752 | tf_op jit(solution)/shard_map/all_to_all | solution.py:40
  37.0 14.7 %collective-permute-start.3 = (bf16[768,384]{1,0:T(8,128)(2,1)S(1)}, bf16[768,384]{1,0:T(8,128)(2,1)S(1)}, u32[]{:S(2)}, u32[]{:S(2)}) collective-permute-start(bf16[768,384]{1,0:T(8,128)(2,1)S(1)} %copy-done), channel_id=1, source_target_pairs={{0,8},{8,0},{16,24},{24,16},{32,40},{40,32},{48,56},{56,48},{64,72... | collective-permute-start | bytes 1769480 | tf_op jit(solution)/shard_map/ppermute | solution.py:48
  48.0 13.1 %all-to-all-start.2 = ((bf16[8,16,768]{2,1,0:T(8,128)(2,1)}), bf16[8,16,768]{2,1,0:T(8,128)(2,1)S(1)}, u32[]{:S(2)}, u32[]{:S(2)}) async-start(bf16[8,16,768]{2,1,0:T(8,128)(2,1)} %shard_map.139), calls=%async_computation.2 | async-start | bytes 393216 | tf_op jit(solution)/shard_map/all_to_all | solution.py:40
  77.3 13.1 %all-to-all-start.4 = ((bf16[8,16,768]{2,1,0:T(8,128)(2,1)}), bf16[8,16,768]{2,1,0:T(8,128)(2,1)S(1)}, u32[]{:S(2)}, u32[]{:S(2)}) async-start(bf16[8,16,768]{2,1,0:T(8,128)(2,1)} %shard_map.141), calls=%async_computation.4 | async-start | bytes 393216 | tf_op jit(solution)/shard_map/all_to_all | solution.py:40
  92.6 20.3 %all-to-all-start.5 = ((bf16[8,16,6144]{2,1,0:T(8,128)(2,1)}), bf16[8,16,6144]{2,1,0:T(8,128)(2,1)S(1)}, u32[]{:S(2)}, u32[]{:S(2)}) async-start(bf16[8,16,6144]{2,1,0:T(8,128)(2,1)} %get-tuple-element.11), calls=%async_computation.5 | async-start | bytes 3145728 | tf_op jit(solution)/shard_map/all_to_all | solution.py:44
